TPU v7x, 256 devices: a whole 4x4x8 slice. The times are simulated.
256 devices in a mesh: paper: 32 (over x_lo, z, core), type: 8 (over y, x_hi).
Axes of the slice: x: 4 (x_hi: 2, x_lo: 2; x = x_hi * 2 + x_lo), y: 4, z: 8, core: 2. Of those that a mesh axis runs over, the one named last changes fastest.
Arguments:
- papers: bfloat16 [131072, 512], P(('paper', 'type')), may hold values from -6 to 6
- cited_rows: bfloat16 [4096, 512], P('paper'), may hold values from -6 to 6
- entities: bfloat16 [1024, 512], P('type'), may hold values from -6 to 6
- entity_kinds: int32 [1024], P('type'), may hold values from 0 to 1
- query_weight: bfloat16 [512, 512], replicated, may hold values from -0.25 to 0.25
- key_weight: bfloat16 [3, 512, 512], replicated, may hold values from -0.25 to 0.25
- value_weight: bfloat16 [3, 512, 512], replicated, may hold values from -0.25 to 0.25
- attention_rel: bfloat16 [4, 8, 64, 64], replicated, may hold values from -0.75 to 0.75
- message_rel: bfloat16 [4, 8, 64, 64], replicated, may hold values from -0.75 to 0.75
- relation_prior: float32 [4, 8], replicated, may hold values from 0.5 to 2.5
- output_weight: bfloat16 [512, 512], replicated, may hold values from -0.25 to 0.25
- skip_gate: float32 [1], replicated, may hold values from -1 to 1
- norm_gain: float32 [512], replicated, may hold values from 0.5 to 1.5
- cite_pattern: int32 [1024, 8, 128, 128], P(('paper', 'type')), may hold values from 0 to 1, as said below
- cite_tiles: int32 [1024, 8], P(('paper', 'type')), may hold values from 0 to 31, as said below
- cite_counts: int32 [1024, 8], P(('paper', 'type')), may hold values from 0 to 16384, as said below
- entity_pattern: int32 [1024, 2, 128, 128], P(('paper', 'type')), may hold values from 0 to 1, as said below
- entity_tiles: int32 [1024, 2], P(('paper', 'type')), may hold values from 0 to 7, as said below
- entity_counts: int32 [1024, 2], P(('paper', 'type')), may hold values from 0 to 16384, as said below
Outputs:
- updated: bfloat16 [131072, 512], P(('paper', 'type'))
Inputs may be any that keep to these rules, and one draw needn't show every extreme that they name: `cite_pattern`: entry [a, k, p, c] is 1 where paper 128 * a + p has an edge from source 128 * cite_tiles[a, k] + c, else 0. A tile of papers uses its first 8, 4, 2 or 1 slots (at least one), the same number for all tiles of one device's papers; later slots are all zero. `cite_tiles`: the slots of one tile name distinct tiles. `cite_counts`: the number of ones in the slot's block. `entity_pattern`: as cite_pattern, with sources 128 * entity_tiles[a, k] + c; a tile uses its first 1 to 2 slots, later slots are all zero. `entity_tiles`: the slots of one tile name distinct tiles. `entity_counts`: the number of ones in the slot's block.
All inputs are finite; a program needn't handle non-finite values.
Results may differ from a plain program's by a relative error of at most 0.0087.
Values may be sent and summed in bfloat16 or wider, within the bound.
No kernel may reach another device: no remote copies, remote signals or barrier semaphores. Data moves between devices by JAX's collectives and lax.ppermute only.
A program may use at most 128 MiB of HBM per device.

v0:
```python
import math

import jax
import jax.numpy as jnp
from jax import lax
from jax.sharding import PartitionSpec as P

CAP = 20.0


def head_split(matrix, head_count):
    return matrix.reshape(matrix.shape[0], head_count, matrix.shape[1] // head_count)


def relate(raw_rows, weight):
    head_count = weight.shape[0]
    mapped = jnp.einsum(
        "nhd,hde->nhe", head_split(raw_rows, head_count), weight, preferred_element_type=jnp.float32
    )
    return mapped.reshape(raw_rows.shape)


def project(source_rows, weight):
    return jnp.dot(source_rows, weight, preferred_element_type=jnp.float32).astype(jnp.bfloat16)


def cited_pairs(source_rows, key_weight, value_weight, attention_rel, message_rel):
    key_rows = relate(project(source_rows, key_weight[0]), attention_rel[0]).astype(jnp.bfloat16)
    value_rows = relate(project(source_rows, value_weight[0]), message_rel[0]).astype(jnp.bfloat16)
    return (key_rows, value_rows)


def entity_side(source_rows, kind_ids, key_weight, value_weight, attention_rel, message_rel):
    author = (kind_ids == 0)[:, None]
    key_raw = jnp.where(
        author,
        jnp.dot(source_rows, key_weight[1], preferred_element_type=jnp.float32),
        jnp.dot(source_rows, key_weight[2], preferred_element_type=jnp.float32),
    ).astype(jnp.bfloat16)
    value_raw = jnp.where(
        author,
        jnp.dot(source_rows, value_weight[1], preferred_element_type=jnp.float32),
        jnp.dot(source_rows, value_weight[2], preferred_element_type=jnp.float32),
    ).astype(jnp.bfloat16)
    key_rows = jnp.where(
        author, relate(key_raw, attention_rel[1]), relate(key_raw, attention_rel[2])
    ).astype(jnp.bfloat16)
    value_rows = jnp.where(
        author, relate(value_raw, message_rel[1]), relate(value_raw, message_rel[2])
    ).astype(jnp.bfloat16)
    return (key_rows, value_rows)


def kind_scales(kind_ids, relation_prior, inv_root):
    author = (kind_ids == 0)[:, None]
    return jnp.where(author, relation_prior[1][None, :], relation_prior[2][None, :]) * inv_root


def own_term(query_heads, own_key, own_value, scale):
    head_count = query_heads.shape[1]
    own_dot = jnp.sum(
        query_heads.astype(jnp.float32) * head_split(own_key, head_count).astype(jnp.float32),
        axis=2,
    )
    weights = jnp.exp(CAP * jnp.tanh(own_dot * scale / CAP))
    rounded = lax.optimization_barrier(weights.astype(jnp.bfloat16)).astype(jnp.float32)
    return (rounded[:, :, None] * head_split(own_value, head_count).astype(jnp.float32), weights)


def dense_live(pattern, tile_ids, counts, source_count):
    chosen = (tile_ids[:, :, None] == jnp.arange(source_count, dtype=jnp.int32)[None, None, :]) & (
        counts[:, :, None] > 0
    )
    spread = jnp.einsum(
        "ikj,ikac->iajc",
        chosen.astype(jnp.bfloat16),
        pattern.astype(jnp.bfloat16),
        preferred_element_type=jnp.float32,
    )
    return (
        spread.reshape(pattern.shape[0] * pattern.shape[2], source_count * pattern.shape[3]) > 0.5
    )


def attend(running, query_heads, key_rows, value_rows, scales, live_mask):
    head_count = query_heads.shape[1]
    products = jnp.einsum(
        "thd,shd->hts",
        query_heads,
        head_split(key_rows, head_count),
        preferred_element_type=jnp.float32,
    )
    scores = products * scales.T[:, None, :]
    scores = CAP * jnp.tanh(scores / CAP)
    weights = jnp.where(live_mask[None, :, :], jnp.exp(scores), 0.0)
    numerator, denominator = running
    numerator = numerator + jnp.einsum(
        "hts,shd->thd",
        weights.astype(jnp.bfloat16),
        head_split(value_rows, head_count),
        preferred_element_type=jnp.float32,
    )
    denominator = denominator + jnp.sum(weights, axis=2).T
    return (numerator, denominator)


def sweep_dense(running, query_heads, key_rows, value_rows, scales, live_mask):
    row_count = key_rows.shape[0]
    block_rows = math.gcd(row_count, 512)
    block_count = row_count // block_rows

    def single_block(offset, state):
        part_keys = lax.dynamic_slice_in_dim(key_rows, offset, block_rows, 0)
        part_values = lax.dynamic_slice_in_dim(value_rows, offset, block_rows, 0)
        part_scales = lax.dynamic_slice_in_dim(scales, offset, block_rows, 0)
        part_live = lax.dynamic_slice_in_dim(live_mask, offset, block_rows, 1)
        return attend(state, query_heads, part_keys, part_values, part_scales, part_live)

    return lax.fori_loop(
        0, block_count, lambda position, state: single_block(position * block_rows, state), running
    )


def per_device(
    papers,
    cited_rows,
    entities,
    entity_kinds,
    query_weight,
    key_weight,
    value_weight,
    attention_rel,
    message_rel,
    relation_prior,
    output_weight,
    skip_gate,
    norm_gain,
    cite_pattern,
    cite_tiles,
    cite_counts,
    entity_pattern,
    entity_tiles,
    entity_counts,
):
    head_count = relation_prior.shape[1]
    model_width = papers.shape[1]
    inv_root = 1.0 / math.sqrt(model_width // head_count)
    tile_size = cite_pattern.shape[2]
    query_heads = head_split(project(papers, query_weight), head_count)
    own_keys = relate(project(papers, key_weight[0]), attention_rel[3]).astype(jnp.bfloat16)
    own_values = relate(project(papers, value_weight[0]), message_rel[3]).astype(jnp.bfloat16)
    running = own_term(query_heads, own_keys, own_values, relation_prior[3] * inv_root)
    cite_sources = cited_rows.shape[0] * lax.axis_size("paper") // tile_size
    entity_sources = entities.shape[0] * lax.axis_size("type") // tile_size
    cite_live = dense_live(cite_pattern, cite_tiles, cite_counts, cite_sources)
    entity_live = dense_live(entity_pattern, entity_tiles, entity_counts, entity_sources)
    cite_scale = relation_prior[0] * inv_root

    def sweep_rows(state, key_rows, value_rows, scales, live_mask):
        return sweep_dense(state, query_heads, key_rows, value_rows, scales, live_mask)

    cite_keys, cite_values = cited_pairs(
        cited_rows, key_weight, value_weight, attention_rel, message_rel
    )
    key_rows = lax.all_gather(cite_keys, "paper", axis=0, tiled=True)
    value_rows = lax.all_gather(cite_values, "paper", axis=0, tiled=True)
    row_count = key_rows.shape[0]
    scales = jnp.broadcast_to(cite_scale[None, :], (row_count, head_count))
    live_mask = cite_live
    running = sweep_rows(running, key_rows, value_rows, scales, live_mask)
    entity_keys, entity_values = entity_side(
        entities, entity_kinds, key_weight, value_weight, attention_rel, message_rel
    )
    key_rows = lax.all_gather(entity_keys, "type", axis=0, tiled=True)
    value_rows = lax.all_gather(entity_values, "type", axis=0, tiled=True)
    kind_ids = lax.all_gather(entity_kinds, "type", axis=0, tiled=True)
    live_mask = entity_live
    scales = kind_scales(kind_ids, relation_prior, inv_root)
    running = sweep_rows(running, key_rows, value_rows, scales, live_mask)
    numerator, denominator = running
    mixed = numerator / denominator[:, :, None]
    hidden = jax.nn.gelu(mixed, approximate=False).reshape(papers.shape).astype(jnp.bfloat16)
    projected = jnp.dot(hidden, output_weight, preferred_element_type=jnp.float32)
    alpha = jax.nn.sigmoid(skip_gate[0])
    blended = alpha * projected + (1.0 - alpha) * papers.astype(jnp.float32)
    centre = jnp.mean(blended, axis=1, keepdims=True)
    spread = jnp.mean(jnp.square(blended - centre), axis=1, keepdims=True)
    return ((blended - centre) * lax.rsqrt(spread + 1e-05) * norm_gain).astype(jnp.bfloat16)


def solution(mesh):
    in_specs = (
        P(("paper", "type"), None),
        P("paper", None),
        P("type", None),
        P("type"),
        P(),
        P(),
        P(),
        P(),
        P(),
        P(),
        P(),
        P(),
        P(),
        P(("paper", "type"), None, None, None),
        P(("paper", "type"), None),
        P(("paper", "type"), None),
        P(("paper", "type"), None, None, None),
        P(("paper", "type"), None),
        P(("paper", "type"), None),
    )
    out_specs = P(("paper", "type"), None)
    return jax.shard_map(
        per_device, mesh=mesh, in_specs=in_specs, out_specs=out_specs, check_vma=False
    )
```

profile of v0, /device:TPU:1, one launch (start us, length us, event | category | flops | bytes accessed | tf_op | source)
XLA Modules:
  0.0 305.3 jit_solution(12606027069432902656)
XLA Ops:
  6.5 1.4 convolution_convert_fusion.6
  8.1 1.8 convolution_convert_fusion.8
  10.0 1.5 convolution_convert_fusion.5
  11.6 1.8 convolution_convert_fusion.7
  14.1 1.3 fusion.50
  15.4 1.4 fusion.37
  18.8 1.3 fusion.53
  20.2 1.4 fusion.36
  26.8 1.8 select_convert_fusion
  29.2 2.3 convolution_convert_fusion.3
  31.6 2.4 convolution_convert_fusion.2
  35.0 1.5 convolution_convert_fusion.4
  36.5 1.7 fusion.35
  39.2 2.5 broadcast_compare_fusion
  41.7 3.0 copy.131
  44.7 20.6 %all-gather = s32[8,1,128]{2,1,0:T(1,128)S(1)} all-gather(s32[1,1,128]{2,1,0:T(1,128)S(1)} %bitcast.259), channel_id=1, replica_groups=mesh['paper'=32,'type'=8] {'type'}, dimensions={0}, use_global_device_ids=true | all-gather | bytes 4608 | tf_op jit(solution)/shard_map/all_gather | solution.py:176
  67.3 2.3 fusion.34
  69.6 17.3 %all-gather.6.cloned.1.call-done = bf16[4096,512]{0,1:T(8,128)(2,1)} async-done(((bf16[128,512]{0,1:T(8,128)(2,1)}), bf16[4096,512]{0,1:T(8,128)(2,1)}) %all-gather.6.cloned.1.call-update) | async-done | bytes 4194320 | tf_op jit(solution)/shard_map/all_gather | solution.py:166
  86.9 72.4 %all-gather.8.cloned.1.call-done = bf16[4096,512]{0,1:T(8,128)(2,1)} async-done(((bf16[128,512]{0,1:T(8,128)(2,1)}), bf16[4096,512]{0,1:T(8,128)(2,1)}) %all-gather.8.cloned.1.call-update) | async-done | bytes 4194320 | tf_op jit(solution)/shard_map/all_gather | solution.py:165
  160.0 92.3 %while.30 = (s32[]{:T(128)}, f32[512,8,64]{0,2,1:T(8,128)}, f32[512,8]{0,1:T(8,128)S(1)}, bf16[4096,512]{0,1:T(8,128)(2,1)}, pred[512,4096]{1,0:T(8,128)(4,1)}, ...) while((s32[]{:T(128)}, f32[512,8,64]{0,2,1:T(8,128)}, ...), condition=%wide.region_3.4_spmd, body=%wide.region_1.3_spmd.sunk | while | flops 558104576 | bytes 32637160 | solution.py:119
  163.4 4.5 %fusion.143 = (f32[8,512]{1,0:T(8,128)S(1)}, f32[8,512,512]{2,1,0:T(8,128)S(1)}) fusion(f32[8,512]{1,0:T(8,128)S(1)} %dynamic-slice_bitcast_fusion.4, pred[512,512]{0,1:T(8,128)(4,1)S(1)} %copy.137, bf16[512,8,64]{0,2,1:T(8,128)(2,1)S(1)} %bitcast.234, bf16[512,8,64]{0,2,1:T(8,128)(2,1)} %get-tuple-element.531), kind=kOutput, calls=%fused_computation.1.clone.1 | convolution fusion | flops 278917120 | bytes 9732096 | tf_op jit(solution)/shard_map/while/body/eval_jaxpr/thd,shd->hts/dot_general | solution.py:87
  167.9 2.6 fusion.144
  171.5 1.3 constant_dynamic-slice_fusion.10
  174.9 4.5 %fusion.143 = (f32[8,512]{1,0:T(8,128)S(1)}, f32[8,512,512]{2,1,0:T(8,128)S(1)}) fusion(f32[8,512]{1,0:T(8,128)S(1)} %dynamic-slice_bitcast_fusion.4, pred[512,512]{0,1:T(8,128)(4,1)S(1)} %copy.137, bf16[512,8,64]{0,2,1:T(8,128)(2,1)S(1)} %bitcast.234, bf16[512,8,64]{0,2,1:T(8,128)(2,1)} %get-tuple-element.531), kind=kOutput, calls=%fused_computation.1.clone.1 | convolution fusion | flops 278917120 | bytes 9732096 | tf_op jit(solution)/shard_map/while/body/eval_jaxpr/thd,shd->hts/dot_general | solution.py:87
  179.4 2.6 fusion.144
  183.1 1.3 constant_dynamic-slice_fusion.10
  186.5 4.5 %fusion.143 = (f32[8,512]{1,0:T(8,128)S(1)}, f32[8,512,512]{2,1,0:T(8,128)S(1)}) fusion(f32[8,512]{1,0:T(8,128)S(1)} %dynamic-slice_bitcast_fusion.4, pred[512,512]{0,1:T(8,128)(4,1)S(1)} %copy.137, bf16[512,8,64]{0,2,1:T(8,128)(2,1)S(1)} %bitcast.234, bf16[512,8,64]{0,2,1:T(8,128)(2,1)} %get-tuple-element.531), kind=kOutput, calls=%fused_computation.1.clone.1 | convolution fusion | flops 278917120 | bytes 9732096 | tf_op jit(solution)/shard_map/while/body/eval_jaxpr/thd,shd->hts/dot_general | solution.py:87
  191.0 2.6 fusion.144
  198.0 4.5 %fusion.143 = (f32[8,512]{1,0:T(8,128)S(1)}, f32[8,512,512]{2,1,0:T(8,128)S(1)}) fusion(f32[8,512]{1,0:T(8,128)S(1)} %dynamic-slice_bitcast_fusion.4, pred[512,512]{0,1:T(8,128)(4,1)S(1)} %copy.137, bf16[512,8,64]{0,2,1:T(8,128)(2,1)S(1)} %bitcast.234, bf16[512,8,64]{0,2,1:T(8,128)(2,1)} %get-tuple-element.531), kind=kOutput, calls=%fused_computation.1.clone.1 | convolution fusion | flops 278917120 | bytes 9732096 | tf_op jit(solution)/shard_map/while/body/eval_jaxpr/thd,shd->hts/dot_general | solution.py:87
  202.5 2.6 fusion.144
  206.2 1.3 constant_dynamic-slice_fusion.10
  209.6 4.5 %fusion.143 = (f32[8,512]{1,0:T(8,128)S(1)}, f32[8,512,512]{2,1,0:T(8,128)S(1)}) fusion(f32[8,512]{1,0:T(8,128)S(1)} %dynamic-slice_bitcast_fusion.4, pred[512,512]{0,1:T(8,128)(4,1)S(1)} %copy.137, bf16[512,8,64]{0,2,1:T(8,128)(2,1)S(1)} %bitcast.234, bf16[512,8,64]{0,2,1:T(8,128)(2,1)} %get-tuple-element.531), kind=kOutput, calls=%fused_computation.1.clone.1 | convolution fusion | flops 278917120 | bytes 9732096 | tf_op jit(solution)/shard_map/while/body/eval_jaxpr/thd,shd->hts/dot_general | solution.py:87
  214.0 2.6 fusion.144
  221.1 4.5 %fusion.143 = (f32[8,512]{1,0:T(8,128)S(1)}, f32[8,512,512]{2,1,0:T(8,128)S(1)}) fusion(f32[8,512]{1,0:T(8,128)S(1)} %dynamic-slice_bitcast_fusion.4, pred[512,512]{0,1:T(8,128)(4,1)S(1)} %copy.137, bf16[512,8,64]{0,2,1:T(8,128)(2,1)S(1)} %bitcast.234, bf16[512,8,64]{0,2,1:T(8,128)(2,1)} %get-tuple-element.531), kind=kOutput, calls=%fused_computation.1.clone.1 | convolution fusion | flops 278917120 | bytes 9732096 | tf_op jit(solution)/shard_map/while/body/eval_jaxpr/thd,shd->hts/dot_general | solution.py:87
  225.6 2.6 fusion.144
  232.6 4.5 %fusion.143 = (f32[8,512]{1,0:T(8,128)S(1)}, f32[8,512,512]{2,1,0:T(8,128)S(1)}) fusion(f32[8,512]{1,0:T(8,128)S(1)} %dynamic-slice_bitcast_fusion.4, pred[512,512]{0,1:T(8,128)(4,1)S(1)} %copy.137, bf16[512,8,64]{0,2,1:T(8,128)(2,1)S(1)} %bitcast.234, bf16[512,8,64]{0,2,1:T(8,128)(2,1)} %get-tuple-element.531), kind=kOutput, calls=%fused_computation.1.clone.1 | convolution fusion | flops 278917120 | bytes 9732096 | tf_op jit(solution)/shard_map/while/body/eval_jaxpr/thd,shd->hts/dot_general | solution.py:87
  237.1 2.6 fusion.144
  244.2 4.5 %fusion.143 = (f32[8,512]{1,0:T(8,128)S(1)}, f32[8,512,512]{2,1,0:T(8,128)S(1)}) fusion(f32[8,512]{1,0:T(8,128)S(1)} %dynamic-slice_bitcast_fusion.4, pred[512,512]{0,1:T(8,128)(4,1)S(1)} %copy.137, bf16[512,8,64]{0,2,1:T(8,128)(2,1)S(1)} %bitcast.234, bf16[512,8,64]{0,2,1:T(8,128)(2,1)} %get-tuple-element.531), kind=kOutput, calls=%fused_computation.1.clone.1 | convolution fusion | flops 278917120 | bytes 9732096 | tf_op jit(solution)/shard_map/while/body/eval_jaxpr/thd,shd->hts/dot_general | solution.py:87
  248.6 2.6 fusion.144
  252.3 10.6 %all-gather.12.cloned.1.call-done = bf16[1024,512]{1,0:T(8,128)(2,1)} async-done(((bf16[128,512]{1,0:T(8,128)(2,1)}), bf16[1024,512]{1,0:T(8,128)(2,1)}) %all-gather.12.cloned.1.call-update) | async-done | bytes 1048592 | tf_op jit(solution)/shard_map/all_gather | solution.py:174
  262.9 29.5 %while.31 = (s32[]{:T(128)}, f32[512,8,64]{0,2,1:T(8,128)}, f32[512,8]{0,1:T(8,128)S(1)}, bf16[1024,512]{1,0:T(8,128)(2,1)}, pred[512,1024]{1,0:T(8,128)(4,1)S(1...) while((s32[]{:T(128)}, f32[512,8,64]{0,2,1:T(8,128)}, ...), condition=%wide.region_6.7_spmd, body=%wide.region_4.6_spmd.sunk | while | flops 558104576 | bytes 34734312 | solution.py:119
  262.9 1.3 constant_dynamic-slice_fusion.12
  264.9 6.5 %fusion.149 = (f32[8,512]{1,0:T(8,128)S(1)}, f32[8,512,512]{2,1,0:T(8,128)}) fusion(f32[8,512]{1,0:T(8,128)S(1)} %dynamic-slice_bitcast_fusion.5, pred[512,512]{0,1:T(8,128)(4,1)S(1)} %copy.139, bf16[512,8,64]{0,2,1:T(8,128)(2,1)S(1)} %bitcast.235, bf16[512,8,64]{0,2,1:T(8,128)(2,1)} %get-tuple-element.567), kind=kOutput, calls=%fused_computation.16.clone.1 | convolution fusion | flops 278917120 | bytes 9732096 | tf_op jit(solution)/shard_map/while/body/eval_jaxpr/thd,shd->hts/dot_general | solution.py:87
  271.6 5.0 %fusion.150 = f32[512,8,64]{0,2,1:T(8,128)S(1)} fusion(f32[512,8,64]{0,2,1:T(8,128)S(1)} %copy-done.3, bf16[512,8,64]{0,2,1:T(8,128)(2,1)S(1)} %bitcast.236, f32[8,512,512]{2,1,0:T(8,128)} %get-tuple-element.499, f32[8,512]{1,0:T(8,128)S(1)} %dynamic-slice_bitcast_fusion.5, pred[512,512]{0,1:T(8,128)(4,1)S(1)} %copy.139), kind=kOutput, calls=%fused_computation.21.clone.1 | convolution fusion | flops 279183360 | bytes 11288576 | tf_op jit(solution)/shard_map/while/body/eval_jaxpr/hts,shd->thd/dot_general | solution.py:97
  279.6 6.5 %fusion.149 = (f32[8,512]{1,0:T(8,128)S(1)}, f32[8,512,512]{2,1,0:T(8,128)}) fusion(f32[8,512]{1,0:T(8,128)S(1)} %dynamic-slice_bitcast_fusion.5, pred[512,512]{0,1:T(8,128)(4,1)S(1)} %copy.139, bf16[512,8,64]{0,2,1:T(8,128)(2,1)S(1)} %bitcast.235, bf16[512,8,64]{0,2,1:T(8,128)(2,1)} %get-tuple-element.567), kind=kOutput, calls=%fused_computation.16.clone.1 | convolution fusion | flops 278917120 | bytes 9732096 | tf_op jit(solution)/shard_map/while/body/eval_jaxpr/thd,shd->hts/dot_general | solution.py:87
  286.3 5.0 %fusion.150 = f32[512,8,64]{0,2,1:T(8,128)S(1)} fusion(f32[512,8,64]{0,2,1:T(8,128)S(1)} %copy-done.3, bf16[512,8,64]{0,2,1:T(8,128)(2,1)S(1)} %bitcast.236, f32[8,512,512]{2,1,0:T(8,128)} %get-tuple-element.499, f32[8,512]{1,0:T(8,128)S(1)} %dynamic-slice_bitcast_fusion.5, pred[512,512]{0,1:T(8,128)(4,1)S(1)} %copy.139), kind=kOutput, calls=%fused_computation.21.clone.1 | convolution fusion | flops 279183360 | bytes 11288576 | tf_op jit(solution)/shard_map/while/body/eval_jaxpr/hts,shd->thd/dot_general | solution.py:97
  292.4 3.4 %fusion.40 = bf16[512,8,64]{0,2,1:T(8,128)(2,1)S(1)} fusion(f32[512,8,64]{0,2,1:T(8,128)} %get-tuple-element.287, f32[512,8]{0,1:T(8,128)S(1)} %get-tuple-element.288), kind=kLoop, calls=%fused_computation.59 | loop fusion | flops 17301504 | bytes 1589248 | tf_op jit(solution)/shard_map/convert_element_type | solution.py:182
  295.8 1.6 fusion.100
  (154 shorter events, 50.5 us)
Async XLA Ops:
  6.5 289.3 %copy-start = (bf16[512,512]{1,0:T(8,128)(2,1)S(1)}, bf16[512,512]{1,0:T(8,128)(2,1)}, u32[]{:S(2)}) copy-start(bf16[512,512]{1,0:T(8,128)(2,1)} %param.33) | copy-start | bytes 1572868
  6.5 22.7 %copy-start.6 = (bf16[512,512]{1,0:T(8,128)(2,1)S(1)}, bf16[512,512]{1,0:T(8,128)(2,1)}, u32[]{:S(2)}) copy-start(bf16[512,512]{1,0:T(8,128)(2,1)} %param.23) | copy-start | bytes 1572868
  6.5 28.4 %copy-start.11 = (f32[4,8]{1,0:T(4,128)S(1)}, f32[4,8]{1,0:T(4,128)}, u32[]{:S(2)}) copy-start(f32[4,8]{1,0:T(4,128)} %param.32) | copy-start | bytes 388
  6.5 80.4 %all-gather.6.cloned.1.call-start = ((), (), s32[]{:S(2)}) async-start(), calls=%async_computation | async-start | bytes 4325376 | tf_op jit(solution)/shard_map/all_gather | solution.py:166
  9.9 28.4 %copy-start.7 = (s32[4,8,128,128]{3,2,1,0:T(8,128)S(1)}, s32[4,8,128,128]{3,2,1,0:T(8,128)}, u32[]{:S(2)}) copy-start(s32[4,8,128,128]{3,2,1,0:T(8,128)} %param.36) | copy-start | bytes 6291460
  9.9 149.3 %all-gather.8.cloned.1.call-start = ((), (), s32[]{:S(2)}) async-start(), calls=%async_computation.1 | async-start | bytes 4325376 | tf_op jit(solution)/shard_map/all_gather | solution.py:165
  13.4 239.0 %all-gather.10.cloned.1.call-start = ((), (), s32[]{:S(2)}) async-start(), calls=%async_computation.2 | async-start | bytes 1179648 | tf_op jit(solution)/shard_map/all_gather | solution.py:175
  28.6 234.3 %all-gather.12.cloned.1.call-start = ((), (), s32[]{:S(2)}) async-start(), calls=%async_computation.3 | async-start | bytes 1179648 | tf_op jit(solution)/shard_map/all_gather | solution.py:174
  36.5 1.7 copy-start.5
  39.2 5.6 %copy-start.13 = (s32[128]{0:T(128)S(1)}, s32[128]{0:T(128)}, u32[]{:S(2)}) copy-start(s32[128]{0:T(128)} %param.26) | copy-start | bytes 1540
  39.2 26.1 %copy-start.8 = (s32[4,2,128,128]{3,2,1,0:T(8,128)S(1)}, s32[4,2,128,128]{3,2,1,0:T(8,128)}, u32[]{:S(2)}) copy-start(s32[4,2,128,128]{3,2,1,0:T(8,128)} %param.39) | copy-start | bytes 1572868
  39.2 26.2 %copy-start.12 = (s32[4,2]{0,1:T(2,128)S(1)}, s32[4,2]{0,1:T(2,128)}, u32[]{:S(2)}) copy-start(s32[4,2]{0,1:T(2,128)} %param.40) | copy-start | bytes 100
  39.2 26.3 %copy-start.14 = (s32[4,2]{0,1:T(2,128)S(1)}, s32[4,2]{0,1:T(2,128)}, u32[]{:S(2)}) copy-start(s32[4,2]{0,1:T(2,128)} %param.41) | copy-start | bytes 100
  41.7 25.5 %copy-start.9 = (bf16[512,512]{0,1:T(8,128)(2,1)S(1)}, bf16[512,512]{0,1:T(8,128)(2,1)}, u32[]{:S(2)}) copy-start(bf16[512,512]{0,1:T(8,128)(2,1)} %convolution_convert_fusion.2) | copy-start | bytes 1572868
  163.4 4.5 %copy-start.1 = (f32[512,8,64]{0,2,1:T(8,128)S(1)}, f32[512,8,64]{0,2,1:T(8,128)}, u32[]{:S(2)}) copy-start(f32[512,8,64]{0,2,1:T(8,128)} %get-tuple-element.514) | copy-start | bytes 3145732 | tf_op jit(solution)/shard_map/while
  170.5 1.0 copy-start.2
  174.9 4.5 %copy-start.1 = (f32[512,8,64]{0,2,1:T(8,128)S(1)}, f32[512,8,64]{0,2,1:T(8,128)}, u32[]{:S(2)}) copy-start(f32[512,8,64]{0,2,1:T(8,128)} %get-tuple-element.514) | copy-start | bytes 3145732 | tf_op jit(solution)/shard_map/while
  182.1 1.0 copy-start.2
  186.5 4.5 %copy-start.1 = (f32[512,8,64]{0,2,1:T(8,128)S(1)}, f32[512,8,64]{0,2,1:T(8,128)}, u32[]{:S(2)}) copy-start(f32[512,8,64]{0,2,1:T(8,128)} %get-tuple-element.514) | copy-start | bytes 3145732 | tf_op jit(solution)/shard_map/while
  193.6 1.0 copy-start.2
  198.0 4.5 %copy-start.1 = (f32[512,8,64]{0,2,1:T(8,128)S(1)}, f32[512,8,64]{0,2,1:T(8,128)}, u32[]{:S(2)}) copy-start(f32[512,8,64]{0,2,1:T(8,128)} %get-tuple-element.514) | copy-start | bytes 3145732 | tf_op jit(solution)/shard_map/while
  205.1 1.0 copy-start.2
  209.6 4.5 %copy-start.1 = (f32[512,8,64]{0,2,1:T(8,128)S(1)}, f32[512,8,64]{0,2,1:T(8,128)}, u32[]{:S(2)}) copy-start(f32[512,8,64]{0,2,1:T(8,128)} %get-tuple-element.514) | copy-start | bytes 3145732 | tf_op jit(solution)/shard_map/while
  216.7 1.0 copy-start.2
  221.1 4.5 %copy-start.1 = (f32[512,8,64]{0,2,1:T(8,128)S(1)}, f32[512,8,64]{0,2,1:T(8,128)}, u32[]{:S(2)}) copy-start(f32[512,8,64]{0,2,1:T(8,128)} %get-tuple-element.514) | copy-start | bytes 3145732 | tf_op jit(solution)/shard_map/while
  228.2 1.0 copy-start.2
  232.6 4.5 %copy-start.1 = (f32[512,8,64]{0,2,1:T(8,128)S(1)}, f32[512,8,64]{0,2,1:T(8,128)}, u32[]{:S(2)}) copy-start(f32[512,8,64]{0,2,1:T(8,128)} %get-tuple-element.514) | copy-start | bytes 3145732 | tf_op jit(solution)/shard_map/while
  239.8 1.0 copy-start.2
  244.2 4.5 %copy-start.1 = (f32[512,8,64]{0,2,1:T(8,128)S(1)}, f32[512,8,64]{0,2,1:T(8,128)}, u32[]{:S(2)}) copy-start(f32[512,8,64]{0,2,1:T(8,128)} %get-tuple-element.514) | copy-start | bytes 3145732 | tf_op jit(solution)/shard_map/while
  251.3 1.0 copy-start.2
  262.9 34.7 %copy-start.10 = (f32[512]{0:T(512)S(1)}, f32[512]{0:T(512)}, u32[]{:S(2)}) copy-start(f32[512]{0:T(512)} %param.35) | copy-start | bytes 6148
  264.9 6.7 %copy-start.3 = (f32[512,8,64]{0,2,1:T(8,128)S(1)}, f32[512,8,64]{0,2,1:T(8,128)}, u32[]{:S(2)}) copy-start(f32[512,8,64]{0,2,1:T(8,128)} %get-tuple-element.550) | copy-start | bytes 3145732 | tf_op jit(solution)/shard_map/while
  276.6 1.0 copy-start.4
  279.6 6.7 %copy-start.3 = (f32[512,8,64]{0,2,1:T(8,128)S(1)}, f32[512,8,64]{0,2,1:T(8,128)}, u32[]{:S(2)}) copy-start(f32[512,8,64]{0,2,1:T(8,128)} %get-tuple-element.550) | copy-start | bytes 3145732 | tf_op jit(solution)/shard_map/while
  291.4 1.0 copy-start.4
Sparse Core Ops, SparseCore 0:
  10.0 76.8 all-gather.5
  88.7 70.5 all-gather.7
  161.9 48.1 all-gather.9
  212.6 50.2 all-gather.11
where the time goes:
time: 307 us; the launch traced here: 305 us
  matrix products  111 us (36%)
  waiting for transfers between devices  101 us (33%)
  local copies, waits for them, and re-layouts  50.6 us (16%)
  blocking collectives  20.6 us (7%)
  between operations  14.1 us (5%)
  other arithmetic  7.42 us (2%)
    all_gather x1, waiting for transfers between devices, per_device(): key_rows = lax.all_gather(cite_keys, 'paper', axis=0, tiled=True)  72.4 us
    dot_general x10, matrix products, attend(): jnp.einsum('thd,shd->hts', query_heads, head_split(key_rows, head_count),...  48.6 us
    dot_general x10, matrix products, attend(): jnp.einsum('hts,shd->thd', weights.astype(jnp.bfloat16), head_split(value...  31.2 us
    all_gather x1, blocking collectives, per_device(): kind_ids = lax.all_gather(entity_kinds, 'type', axis=0, tiled=True)  20.6 us
    all_gather x1, waiting for transfers between devices, per_device(): value_rows = lax.all_gather(cite_values, 'paper', axis=0, tiled=True)  17.3 us
    dynamic_slice x12, local copies, waits for them, and re-layouts, single_block(): part_keys = lax.dynamic_slice_in_dim(key_rows, offset, block_rows, 0)  13.2 us
    dot_general x8, matrix products, relate(): jnp.einsum('nhd,hde->nhe', head_split(raw_rows, head_count), weight, pref...  12.1 us
    dynamic_slice x20, local copies, waits for them, and re-layouts, single_block(): part_live = lax.dynamic_slice_in_dim(live_mask, offset, block_rows, 1)  11.9 us
  transfers between devices with their start and end apart: 4, of which 3 were waited for; matrix products, arithmetic and copies ran while one was open for 40% of the time, Pallas kernels for 0%

commit v1 on v0

v1 whole, which is shorter than its diff:
```python
import functools
import math

import jax
import jax.numpy as jnp
from jax import lax
from jax.experimental import pallas as pl
from jax.experimental.pallas import tpu as pltpu
from jax.sharding import PartitionSpec as P

CAP = 20.0
D = 512
HEADS = 8
TILE = 128
PAIRS = 4
F32 = jnp.float32
BF16 = jnp.bfloat16
LOG2E = 1.4426950408889634
ZS, YS, XS = 8, 4, 4
VMEM_LIMIT = 56 * 1024 * 1024


def device_index(x, y, z, core):
    x_hi, x_lo = x // 2, x % 2
    return (x_lo * 16 + z * 2 + core) * 8 + (y * 2 + x_hi)


def permutation(move):
    pairs = []
    for x in range(XS):
        for y in range(YS):
            for z in range(ZS):
                for core in range(2):
                    tx, ty, tz, tc = move(x, y, z, core)
                    pairs.append(
                        (device_index(x, y, z, core), device_index(tx % XS, ty % YS, tz % ZS, tc))
                    )
    return pairs


def send(value, move):
    return lax.ppermute(value, ("paper", "type"), permutation(move))


def core_move(x, y, z, c):
    return (x, y, z, 1 - c)


def z_move(x, y, z, c):
    return (x, y, z + (1 if c == 0 else -1), c)


def x_move(x, y, z, c):
    return (x + (-1 if c == 0 else 1), y, z, c)


def hi_move(x, y, z, c):
    return ({0: 3, 3: 0, 1: 2, 2: 1}[x], y, z, c)


def y_move(step):
    return lambda x, y, z, c: (x, y - step, z, c)


def dot(a, b):
    return lax.dot_general(a, b, (((1,), (0,)), ((), ())), preferred_element_type=F32)


def dot_t(a, b):
    return lax.dot_general(a, b, (((1,), (1,)), ((), ())), preferred_element_type=F32)


def iota(shape, dim):
    return lax.broadcasted_iota(jnp.int32, shape, dim)


def low_half(rows):
    return (iota((rows, TILE), 1) & 64) == 0


def own_kernel(
    papers, query_w, key_w, value_w, att, msg, prior, q2, num0, den0, cite_w, ent_w, blocks, own_w
):
    lane = iota((64, 256), 1)
    row = iota((64, 256), 0)
    for i in range(4):
        place = (lane == row + 64 * i).astype(F32).astype(BF16)
        for t, rel in enumerate((att, msg)):
            for r in range(4):
                for g in range(2):
                    blocks[t, r, g, 64 * i : 64 * i + 64, :] = dot(rel[r, 4 * g + i], place).astype(
                        BF16
                    )
    for t, weight in enumerate((key_w, value_w)):
        for g in range(2):
            cols = slice(256 * g, 256 * g + 256)
            base = weight[0, :, cols]
            own_w[:, 512 * t + 256 * g : 512 * t + 256 * g + 256] = dot(
                base, blocks[t, 3, g]
            ).astype(BF16)
            cite_w[:, 512 * t + 256 * g : 512 * t + 256 * g + 256] = dot(
                base, blocks[t, 0, g]
            ).astype(BF16)
            for u in range(2):
                ent_w[512 * u : 512 * u + 512, 512 * t + 256 * g : 512 * t + 256 * g + 256] = dot(
                    weight[1 + u, :, cols], blocks[t, 1 + u, g]
                ).astype(BF16)
    half = low_half(D)
    zero = jnp.zeros((D, TILE), BF16)
    sums = ((iota((TILE, TILE), 0) & 64) == (iota((TILE, TILE), 1) & 64)).astype(F32).astype(BF16)
    rows = papers[...]
    for j in range(PAIRS):
        cols = slice(TILE * j, TILE * j + TILE)
        q = dot(rows, query_w[:, cols]).astype(BF16)
        k = dot(rows, own_w[:, cols]).astype(BF16)
        v = dot(rows, own_w[:, 512 + TILE * j : 512 + TILE * j + TILE]).astype(BF16)
        q2[0, :, cols] = jnp.where(half, q, zero)
        q2[1, :, cols] = jnp.where(half, zero, q)
        product = q.astype(F32) * k.astype(F32)
        high = product.astype(BF16)
        low = (product - high.astype(F32)).astype(BF16)
        score = dot(high, sums) + dot(low, sums)
        scale = jnp.where(low_half(1), prior[3, 2 * j], prior[3, 2 * j + 1]) * (0.125 / CAP)
        weight = jnp.exp2(jnp.tanh(score * scale) * (CAP * LOG2E))
        den0[:, cols] = weight
        num0[:, cols] = weight.astype(BF16).astype(F32) * v.astype(F32)


def attend_kernel(
    cite_tiles,
    cite_counts,
    entity_tiles,
    entity_counts,
    prior,
    gate,
    part0,
    part1,
    part2,
    part3,
    ent0,
    ent1,
    ent2,
    ent3,
    q2,
    num0,
    den0,
    cite_w,
    ent_w,
    cite_pattern,
    entity_pattern,
    papers,
    output_w,
    gain,
    updated,
    keys,
    values,
    ekeys,
    evalues,
    escale,
    acc,
    slots,
):
    paper_at = lax.axis_index("paper")
    type_at = lax.axis_index("type")
    x_lo, z_at, core = paper_at // 16, (paper_at // 2) % ZS, paper_at % 2
    half = low_half(1)
    one = jnp.ones((1, TILE), BF16)

    def put_values(ref, at, j, v):
        cols = slice(TILE * j, TILE * j + TILE)
        ref[0, at, cols] = jnp.where(half, v, one)
        ref[1, at, cols] = jnp.where(half, one, v)

    for index, part in enumerate((part0, part1, part2, part3)):
        tile_core = core if index % 2 == 0 else 1 - core
        tile_x = x_lo if index < 2 else 1 - x_lo
        step = 2 * tile_core - 1
        order = [(0, 0)] + [(s, o) for s in (1, 2, 3) for o in (0, 1)] + [(4, 0)]
        places = []
        for s, other in order:
            z = (z_at + s * step + ZS) % ZS
            c = tile_core if other == 0 else 1 - tile_core
            places.append(pl.multiple_of((tile_x * 16 + z * 2 + c) * TILE, TILE))
        rows = part[...]
        for n in range(4):
            made = dot(rows, cite_w[:, 256 * n : 256 * n + 256]).astype(BF16)
            for t in range(8):
                at = pl.ds(places[t], TILE)
                block = made[TILE * t : TILE * t + TILE]
                if n < 2:
                    keys[at, 256 * n : 256 * n + 256] = block
                else:
                    put_values(values, at, 2 * (n - 2), block[:, :TILE])
                    put_values(values, at, 2 * (n - 2) + 1, block[:, TILE:])
    y_at, hi_at = type_at // 2, type_at % 2
    pick = (iota((8, TILE), 1) == 0).astype(F32).astype(BF16)
    for s, part in enumerate((ent0, ent1, ent2, ent3)):
        places = []
        for other in range(2):
            y = (y_at + (0, 1, 3, 2)[s]) % YS
            hi = hi_at if other == 0 else 1 - hi_at
            places.append(y * 2 + hi)
        rows = part[:, :D]
        kind = part[:, D : D + TILE]
        kind4 = jnp.concatenate([kind] * 4, axis=1)
        split = jnp.concatenate([rows * (1 - kind4), rows * kind4], axis=1)
        for n in range(4):
            made = dot(split, ent_w[:, 256 * n : 256 * n + 256]).astype(BF16)
            for t in range(2):
                at = pl.ds(pl.multiple_of(places[t] * TILE, TILE), TILE)
                block = made[TILE * t : TILE * t + TILE]
                if n < 2:
                    ekeys[at, 256 * n : 256 * n + 256] = block
                else:
                    put_values(evalues, at, 2 * (n - 2), block[:, :TILE])
                    put_values(evalues, at, 2 * (n - 2) + 1, block[:, TILE:])
        for t in range(2):
            kind_row = dot_t(pick, kind[TILE * t : TILE * t + TILE])[0:1]
            for h in range(HEADS):
                escale[places[t], h : h + 1, :] = jnp.where(
                    kind_row < 0.5, prior[1, h], prior[2, h]
                ) * (0.125 / CAP)

    alpha = jax.nn.sigmoid(jnp.full((1, D), gate[0], F32))

    def tile_body(a, carry):
        rows = pl.ds(pl.multiple_of(a * TILE, TILE), TILE)
        count = jnp.int32(0)
        for k in range(8):
            slots[count] = k
            count = count + (cite_counts[a, k] > 0).astype(jnp.int32)

        def block_pair(src_k, src_v, t0, t1, mask, scale_of, first):
            at0 = pl.ds(pl.multiple_of(t0 * TILE, TILE), TILE)
            at1 = pl.ds(pl.multiple_of(t1 * TILE, TILE), TILE)
            for j in range(PAIRS):
                cols = slice(TILE * j, TILE * j + TILE)
                kk = jnp.concatenate([src_k[at0, cols], src_k[at1, cols]], axis=0)
                for e in range(2):
                    vv = jnp.concatenate([src_v[e, at0, cols], src_v[e, at1, cols]], axis=0)
                    score = dot_t(q2[e, rows, cols], kk)
                    weight = jnp.exp2(jnp.tanh(score * scale_of(2 * j + e)) * (CAP * LOG2E))
                    weight = weight.astype(BF16) * mask
                    got = dot(weight, vv)
                    if first:
                        acc[e, rows, cols] = got
                    else:
                        acc[e, rows, cols] += got

        def mask_of(pattern, k, live):
            return jnp.where((pattern[a, k] > 0) & live, 1.0, 0.0).astype(BF16)

        e0, e1 = entity_tiles[a, 0], entity_tiles[a, 1]
        mask = jnp.concatenate(
            [mask_of(entity_pattern, k, entity_counts[a, k] > 0) for k in range(2)], axis=1
        )
        block_pair(
            ekeys,
            evalues,
            e0,
            e1,
            mask,
            lambda h: jnp.concatenate([escale[e0, h : h + 1, :], escale[e1, h : h + 1, :]], axis=1),
            True,
        )

        def pair_body(i, carry):
            k0 = slots[2 * i]
            second = 2 * i + 1 < count
            k1 = jnp.where(second, slots[2 * i + 1], k0)
            mask = jnp.concatenate(
                [mask_of(cite_pattern, k0, True), mask_of(cite_pattern, k1, second)], axis=1
            )
            block_pair(
                keys,
                values,
                cite_tiles[a, k0],
                cite_tiles[a, k1],
                mask,
                lambda h: prior[0, h] * (0.125 / CAP),
                False,
            )
            return carry

        lax.fori_loop(0, (count + 1) // 2, pair_body, 0)

        hidden = []
        for j in range(PAIRS):
            cols = slice(TILE * j, TILE * j + TILE)
            even, odd = acc[0, rows, cols], acc[1, rows, cols]
            num = jnp.where(half, even, odd) + num0[rows, cols]
            den = pltpu.roll(jnp.where(half, odd, even), 64, 1) + den0[rows, cols]
            mixed = num / den
            hidden.append((0.5 * mixed * (1.0 + lax.erf(mixed * math.sqrt(0.5)))).astype(BF16))
        projected = dot(jnp.concatenate(hidden, axis=1), output_w[...])
        blended = alpha * projected + (1.0 - alpha) * papers[rows, :].astype(F32)
        centre = jnp.mean(blended, axis=1, keepdims=True)
        blended = blended - centre
        spread = jnp.mean(jnp.square(blended), axis=1, keepdims=True)
        updated[rows, :] = (blended * lax.rsqrt(spread + 1e-05) * gain[...]).astype(BF16)
        return carry

    lax.fori_loop(0, 4, tile_body, 0)


def per_device(
    papers,
    cited_rows,
    entities,
    entity_kinds,
    query_weight,
    key_weight,
    value_weight,
    attention_rel,
    message_rel,
    relation_prior,
    output_weight,
    skip_gate,
    norm_gain,
    cite_pattern,
    cite_tiles,
    cite_counts,
    entity_pattern,
    entity_tiles,
    entity_counts,
):
    vmem = pl.BlockSpec(memory_space=pltpu.VMEM)
    smem = pl.BlockSpec(memory_space=pltpu.SMEM)
    shape = jax.ShapeDtypeStruct

    pair = jnp.concatenate([cited_rows, send(cited_rows, core_move)], axis=0)
    kinds = jnp.broadcast_to(entity_kinds.astype(BF16)[:, None], (TILE, TILE))
    ent_own = jnp.concatenate([entities, kinds], axis=1)
    ent_pair = jnp.concatenate([ent_own, send(ent_own, hi_move)], axis=0)
    z1 = send(pair, z_move)
    ent1 = send(ent_pair, y_move(1))
    ent3 = send(ent_pair, y_move(3))
    z2 = send(z1, z_move)
    ent2 = send(ent_pair, y_move(2))
    z3 = send(z2, z_move)
    z4 = send(z3[:TILE], z_move)
    part0 = jnp.concatenate([cited_rows, z1, z2, z3, z4], axis=0)
    part2 = send(part0, x_move)
    part1 = send(part0, core_move)
    part3 = send(part2, core_move)

    q2, num0, den0, cite_w, ent_w = pl.pallas_call(
        own_kernel,
        out_shape=(
            shape((2, 512, D), BF16),
            shape((512, D), F32),
            shape((512, D), F32),
            shape((D, 2 * D), BF16),
            shape((2 * D, 2 * D), BF16),
        ),
        in_specs=[vmem] * 6 + [smem],
        out_specs=(vmem,) * 5,
        scratch_shapes=[
            pltpu.VMEM((2, 4, 2, 256, 256), BF16),
            pltpu.VMEM((D, 2 * D), BF16),
        ],
        compiler_params=pltpu.CompilerParams(vmem_limit_bytes=VMEM_LIMIT),
        cost_estimate=pl.CostEstimate(flops=4 * 10**9, bytes_accessed=10 * 2**20, transcendentals=0),
        name="own_terms",
    )(papers, query_weight, key_weight, value_weight, attention_rel, message_rel, relation_prior)

    return pl.pallas_call(
        attend_kernel,
        out_shape=shape((512, D), BF16),
        in_specs=[smem] * 6 + [vmem] * 18,
        out_specs=vmem,
        scratch_shapes=[
            pltpu.VMEM((4096, D), BF16),
            pltpu.VMEM((2, 4096, D), BF16),
            pltpu.VMEM((1024, D), BF16),
            pltpu.VMEM((2, 1024, D), BF16),
            pltpu.VMEM((8, HEADS, TILE), F32),
            pltpu.VMEM((2, 512, D), F32),
            pltpu.SMEM((16,), jnp.int32),
        ],
        compiler_params=pltpu.CompilerParams(vmem_limit_bytes=VMEM_LIMIT),
        cost_estimate=pl.CostEstimate(flops=10**10, bytes_accessed=20 * 2**20, transcendentals=10**7),
        name="attend_and_finish",
    )(
        cite_tiles,
        cite_counts,
        entity_tiles,
        entity_counts,
        relation_prior,
        skip_gate,
        part0,
        part1,
        part2,
        part3,
        ent_pair,
        ent1,
        ent3,
        ent2,
        q2,
        num0,
        den0,
        cite_w,
        ent_w,
        cite_pattern,
        entity_pattern,
        papers,
        output_weight,
        norm_gain.reshape(1, D),
    )


def solution(mesh):
    split = P(("paper", "type"))
    in_specs = (
        P(("paper", "type"), None),
        P("paper", None),
        P("type", None),
        P("type"),
        P(),
        P(),
        P(),
        P(),
        P(),
        P(),
        P(),
        P(),
        P(),
        split,
        split,
        split,
        split,
        split,
        split,
    )
    return jax.shard_map(
        per_device, mesh=mesh, in_specs=in_specs, out_specs=P(("paper", "type"), None), check_vma=False
    )
```

time: 307 us -> 109 us (0.36)
  matrix products: 111 us -> 0 us
  waiting for transfers between devices: 101 us -> 25.9 us
  local copies, waits for them, and re-layouts: 50.6 us -> 3.28 us
  starting transfers between devices: 0.13 us -> 39.1 us
  Pallas kernels: 0 us -> 38.4 us
  blocking collectives: 20.6 us -> 0 us
  between operations: 14.1 us -> 0.81 us
  other arithmetic: 7.42 us -> 0.97 us
    dot_general x40 -> x0, matrix products: 111 us -> none  [the longest x10 48.6 us: attend(): jnp.einsum('thd,shd->hts', query_heads, head_split(key_rows, head_count),...]
    all_gather x4 -> x0, waiting for transfers between devices: 100 us -> none  [the longest x1 72.4 us: per_device(): key_rows = lax.all_gather(cite_keys, 'paper', axis=0, tiled=True)]
    ppermute x0 -> x12, starting transfers between devices: none -> 39.1 us  [send(): return lax.ppermute(value, ('paper', 'type'), permutation(move))]
    pallas_call x0 -> x2, Pallas kernels: none -> 38.4 us  [the longest x1 30.1 us: per_device(): pl.pallas_call(attend_kernel, out_shape=shape((512, D), BF16), in_specs=[...]
    ppermute x0 -> x12, waiting for transfers between devices: none -> 25.9 us  [send(): return lax.ppermute(value, ('paper', 'type'), permutation(move))]
    dynamic_slice x34 -> x0, local copies, waits for them, and re-layouts: 25.4 us -> none  [the longest x12 13.2 us: single_block(): part_keys = lax.dynamic_slice_in_dim(key_rows, offset, block_rows, 0)]
    all_gather x1 -> x0, blocking collectives: 20.6 us -> none  [per_device(): kind_ids = lax.all_gather(entity_kinds, 'type', axis=0, tiled=True)]
    while x40 -> x0, local copies, waits for them, and re-layouts: 10.1 us -> none
  transfers between devices with their start and end apart: 4 -> 12, of which waited for: 3 -> 8; matrix products, arithmetic and copies ran while one was open for 40% -> 2% of each run, Pallas kernels for 0% -> 8%
where the time goes in v1:
time: 109 us; the launch traced here: 108 us
  starting transfers between devices  39.1 us (36%)
  Pallas kernels  38.4 us (35%)
  waiting for transfers between devices  25.9 us (24%)
  local copies, waits for them, and re-layouts  3.28 us (3%)
    ppermute x12, starting transfers between devices, send(): return lax.ppermute(value, ('paper', 'type'), permutation(move))  39.1 us
    pallas_call x1, Pallas kernels, per_device(): pl.pallas_call(attend_kernel, out_shape=shape((512, D), BF16), in_specs=[...  30.1 us
    ppermute x12, waiting for transfers between devices, send(): return lax.ppermute(value, ('paper', 'type'), permutation(move))  25.9 us
    pallas_call x1, Pallas kernels, per_device(): pl.pallas_call(own_kernel, out_shape=(shape((2, 512, D), BF16), shape((51...  8.3 us
    unnamed x26, local copies, waits for them, and re-layouts  3.18 us
  transfers between devices with their start and end apart: 12, of which 8 were waited for; matrix products, arithmetic and copies ran while one was open for 2% of the time, Pallas kernels for 8%

profile of v1, /device:TPU:1, one launch (start us, length us, event | category | flops | bytes accessed | tf_op | source)
XLA Modules:
  0.0 108.5 jit_solution(556924743980855529)
XLA Ops:
  0.0 0.0 copy-start.9
  0.0 0.0 copy-start
  0.0 0.0 copy-start.4
  0.0 3.3 %collective-permute-start = (bf16[128,512]{1,0:T(8,128)(2,1)}, bf16[128,512]{1,0:T(8,128)(2,1)S(1)}, u32[]{:S(2)}, u32[]{:S(2)}) collective-permute-start(bf16[128,512]{1,0:T(8,128)(2,1)} %param.20), channel_id=1, source_target_pairs={{0,8},{8,0},{16,24},{24,16},{32,40},{40,32},{48,56},{56,48},{64,72... | collective-permute-start | bytes 393224 | tf_op jit(solution)/shard_map/ppermute | solution.py:42
  3.3 1.2 %collective-permute-done = bf16[128,512]{1,0:T(8,128)(2,1)S(1)} collective-permute-done((bf16[128,512]{1,0:T(8,128)(2,1)}, bf16[128,512]{1,0:T(8,128)(2,1)S(1)}, u32[]{:S(2)}, u32[]{:S(2)}) %collective-permute-start) | collective-permute-done | bytes 131104 | tf_op jit(solution)/shard_map/ppermute | solution.py:42
  4.5 0.9 pad_maximum_fusion.1
  5.5 3.9 %collective-permute-start.1 = (bf16[256,512]{1,0:T(8,128)(2,1)S(1)}, bf16[256,512]{1,0:T(8,128)(2,1)S(1)}, u32[]{:S(2)}, u32[]{:S(2)}) collective-permute-start(bf16[256,512]{1,0:T(8,128)(2,1)S(1)} %pad_maximum_fusion.1), channel_id=1, source_target_pairs={{0,16},{8,120},{16,32},{24,8},{32,48},{40,24},{48,64},{56,40},{64,... | collective-permute-start | bytes 786440 | tf_op jit(solution)/shard_map/ppermute | solution.py:42
  9.4 3.3 %collective-permute-done.1 = bf16[256,512]{1,0:T(8,128)(2,1)S(1)} collective-permute-done((bf16[256,512]{1,0:T(8,128)(2,1)S(1)}, bf16[256,512]{1,0:T(8,128)(2,1)S(1)}, u32[]{:S(2)}, u32[]{:S(2)}) %collective-permute-start.1) | collective-permute-done | bytes 262176 | tf_op jit(solution)/shard_map/ppermute | solution.py:42
  12.7 3.1 %collective-permute-start.2 = (bf16[256,512]{1,0:T(8,128)(2,1)S(1)}, bf16[256,512]{1,0:T(8,128)(2,1)S(1)}, u32[]{:S(2)}, u32[]{:S(2)}) collective-permute-start(bf16[256,512]{1,0:T(8,128)(2,1)S(1)} %collective-permute-done.1), channel_id=1, source_target_pairs={{0,16},{8,120},{16,32},{24,8},{32,48},{40,24},{48,64},{56,40},{64,... | collective-permute-start | bytes 786440 | tf_op jit(solution)/shard_map/ppermute | solution.py:42
  15.8 3.3 %collective-permute-done.2 = bf16[256,512]{1,0:T(8,128)(2,1)S(1)} collective-permute-done((bf16[256,512]{1,0:T(8,128)(2,1)S(1)}, bf16[256,512]{1,0:T(8,128)(2,1)S(1)}, u32[]{:S(2)}, u32[]{:S(2)}) %collective-permute-start.2) | collective-permute-done | bytes 262176 | tf_op jit(solution)/shard_map/ppermute | solution.py:42
  19.1 3.1 %collective-permute-start.3 = (bf16[256,512]{1,0:T(8,128)(2,1)S(1)}, bf16[256,512]{1,0:T(8,128)(2,1)S(1)}, u32[]{:S(2)}, u32[]{:S(2)}) collective-permute-start(bf16[256,512]{1,0:T(8,128)(2,1)S(1)} %collective-permute-done.2), channel_id=1, source_target_pairs={{0,16},{8,120},{16,32},{24,8},{32,48},{40,24},{48,64},{56,40},{64,... | collective-permute-start | bytes 786440 | tf_op jit(solution)/shard_map/ppermute | solution.py:42
  22.3 0.9 constant_dynamic-update-slice_fusion.4
  23.2 2.4 %collective-permute-done.3 = bf16[256,512]{1,0:T(8,128)(2,1)S(1)} collective-permute-done((bf16[256,512]{1,0:T(8,128)(2,1)S(1)}, bf16[256,512]{1,0:T(8,128)(2,1)S(1)}, u32[]{:S(2)}, u32[]{:S(2)}) %collective-permute-start.3) | collective-permute-done | bytes 262176 | tf_op jit(solution)/shard_map/ppermute | solution.py:42
  25.6 3.2 %collective-permute-start.4 = (bf16[128,512]{1,0:T(8,128)(2,1)S(1)}, bf16[128,512]{1,0:T(8,128)(2,1)S(1)}, u32[]{:S(2)}, u32[]{:S(2)}) collective-permute-start(bf16[128,512]{1,0:T(8,128)(2,1)S(1)} %slice.4), channel_id=1, source_target_pairs={{0,16},{8,120},{16,32},{24,8},{32,48},{40,24},{48,64},{56,40},{64,... | collective-permute-start | bytes 393224 | tf_op jit(solution)/shard_map/ppermute | solution.py:42
  28.8 1.9 %collective-permute-done.4 = bf16[128,512]{1,0:T(8,128)(2,1)S(1)} collective-permute-done((bf16[128,512]{1,0:T(8,128)(2,1)S(1)}, bf16[128,512]{1,0:T(8,128)(2,1)S(1)}, u32[]{:S(2)}, u32[]{:S(2)}) %collective-permute-start.4) | collective-permute-done | bytes 131104 | tf_op jit(solution)/shard_map/ppermute | solution.py:42
  30.7 0.0 copy-start.2
  30.7 1.3 %collective-permute-start.6 = (bf16[1024,512]{1,0:T(8,128)(2,1)S(1)}, bf16[1024,512]{1,0:T(8,128)(2,1)S(1)}, u32[]{:S(2)}, u32[]{:S(2)}) collective-permute-start(bf16[1024,512]{1,0:T(8,128)(2,1)S(1)} %constant_dynamic-update-slice_fusion.part0), channel_id=1, source_target_pairs={{0,129},{8,136},{16,145},{24,152},{32,161},{40,168},{48,177},{56,1... | collective-permute-start | bytes 3145736 | tf_op jit(solution)/shard_map/ppermute | solution.py:42
  32.0 6.6 %collective-permute-start.5 = (bf16[1024,512]{1,0:T(8,128)(2,1)S(1)}, bf16[1024,512]{1,0:T(8,128)(2,1)}, u32[]{:S(2)}, u32[]{:S(2)}) collective-permute-start(bf16[1024,512]{1,0:T(8,128)(2,1)S(1)} %constant_dynamic-update-slice_fusion.part0), channel_id=1, source_target_pairs={{0,8},{8,0},{16,24},{24,16},{32,40},{40,32},{48,56},{56,48},{64,72... | collective-permute-start | bytes 3145736 | tf_op jit(solution)/shard_map/ppermute | solution.py:42
  38.7 7.0 %collective-permute-done.6.part2 = bf16[1024,512]{1,0:T(8,128)(2,1)S(1)} collective-permute-done((bf16[1024,512]{1,0:T(8,128)(2,1)S(1)}, bf16[1024,512]{1,0:T(8,128)(2,1)S(1)}, u32[]{:S(2)}, u32[]{:S(2)}) %collective-permute-start.6) | collective-permute-done | bytes 1048608 | tf_op jit(solution)/shard_map/ppermute | solution.py:42
  45.7 0.0 copy-start.5
  45.7 5.3 %collective-permute-start.7 = (bf16[1024,512]{1,0:T(8,128)(2,1)S(1)}, bf16[1024,512]{1,0:T(8,128)(2,1)}, u32[]{:S(2)}, u32[]{:S(2)}) collective-permute-start(bf16[1024,512]{1,0:T(8,128)(2,1)S(1)} %collective-permute-done.6.part2), channel_id=1, source_target_pairs={{0,8},{8,0},{16,24},{24,16},{32,40},{40,32},{48,56},{56,48},{64,72... | collective-permute-start | bytes 3145736 | tf_op jit(solution)/shard_map/ppermute | solution.py:42
  51.0 0.0 copy-done.9
  51.0 0.1 broadcast_in_dim.2
  51.1 0.0 copy-done
  51.1 3.5 %collective-permute-start.8 = (bf16[128,640]{1,0:T(8,128)(2,1)S(1)}, bf16[128,640]{1,0:T(8,128)(2,1)S(1)}, u32[]{:S(2)}, u32[]{:S(2)}) collective-permute-start(bf16[128,640]{1,0:T(8,128)(2,1)S(1)} %pad_maximum_fusion.2), channel_id=1, source_target_pairs={{0,129},{8,137},{16,145},{24,153},{32,161},{40,169},{48,177},{56,1... | collective-permute-start | bytes 491528 | tf_op jit(solution)/shard_map/ppermute | solution.py:42
  55.3 0.0 copy-done.3
  55.3 0.7 copy.20.entity_tiles
  56.0 0.0 copy-done.4
  56.0 0.7 copy.21.entity_counts
  56.6 2.5 %collective-permute-done.8 = bf16[128,640]{1,0:T(8,128)(2,1)S(1)} collective-permute-done((bf16[128,640]{1,0:T(8,128)(2,1)S(1)}, bf16[128,640]{1,0:T(8,128)(2,1)S(1)}, u32[]{:S(2)}, u32[]{:S(2)}) %collective-permute-start.8) | collective-permute-done | bytes 163872 | tf_op jit(solution)/shard_map/ppermute | solution.py:42
  59.2 0.0 copy-start.1
  59.2 3.0 %collective-permute-start.11 = (bf16[256,640]{1,0:T(8,128)(2,1)S(1)}, bf16[256,640]{1,0:T(8,128)(2,1)S(1)}, u32[]{:S(2)}, u32[]{:S(2)}) collective-permute-start(bf16[256,640]{1,0:T(8,128)(2,1)S(1)} %pad_maximum_fusion.ent0), channel_id=1, source_target_pairs={{0,4},{8,12},{16,20},{24,28},{32,36},{40,44},{48,52},{56,60},{64,6... | collective-permute-start | bytes 983048 | tf_op jit(solution)/shard_map/ppermute | solution.py:42
  62.2 0.4 collective-permute-start.10
  62.6 2.3 %collective-permute-start.9 = (bf16[256,640]{1,0:T(8,128)(2,1)S(1)}, bf16[256,640]{1,0:T(8,128)(2,1)S(1)}, u32[]{:S(2)}, u32[]{:S(2)}) collective-permute-start(bf16[256,640]{1,0:T(8,128)(2,1)S(1)} %pad_maximum_fusion.ent0), channel_id=1, source_target_pairs={{0,6},{8,14},{16,22},{24,30},{32,38},{40,46},{48,54},{56,62},{64,7... | collective-permute-start | bytes 983048 | tf_op jit(solution)/shard_map/ppermute | solution.py:42
  64.9 8.3 %own_terms.1 = (bf16[2,512,512]{2,1,0:T(8,128)(2,1)}, f32[512,512]{1,0:T(8,128)}, f32[512,512]{1,0:T(8,128)}, bf16[512,1024]{1,0:T(8,128)(2,1)}, bf16[1024,1024]{1,0:T(8,128)(2,1)}) custom-call(bf16[512,512]{1,0:T(8,128)(2,1)} %papers.3, bf16[512,512]{1,0:T(8,128)(2,1)} %query_w.1, bf16[3,512,512]{2,1,0:T(8,128)(2,1)} %key_w.1, ...), custom_call_target="tpu_custom_call" | custom-call | flops 4000000000 | bytes 10485760 | tf_op jit(solution)/shard_map/own_terms/pallas_call | solution.py:347
  73.2 0.0 copy-done.2
  73.2 0.0 copy-done.5
  73.2 0.0 copy-done.1
  73.2 0.0 collective-permute-done.11.ent3
  73.2 0.0 copy-start.6
  73.3 4.2 %collective-permute-done.10.ent2 = bf16[256,640]{1,0:T(8,128)(2,1)S(1)} collective-permute-done((bf16[256,640]{1,0:T(8,128)(2,1)S(1)}, bf16[256,640]{1,0:T(8,128)(2,1)S(1)}, u32[]{:S(2)}, u32[]{:S(2)}) %collective-permute-start.10) | collective-permute-done | bytes 327712 | tf_op jit(solution)/shard_map/ppermute | solution.py:42
  77.5 0.0 collective-permute-done.9.ent1
  77.5 0.0 collective-permute-done.5.part1
  77.5 0.0 collective-permute-done.7.part3
  77.5 0.0 copy-done.6
  77.5 0.7 copy-done.7
  78.2 0.1 copy-done.8
  78.3 30.1 %attend_and_finish.1 = bf16[512,512]{1,0:T(8,128)(2,1)} custom-call(s32[4,8]{1,0:T(4,128)} %cite_tiles.1, s32[4,8]{1,0:T(4,128)} %cite_counts.1, s32[4,2]{1,0:T(4,128)} %copy.20.entity_tiles, s32[4,2]{1,0:T(4,128)} %copy.21.entity_counts, f32[4,8]{1,0:T(4,128)} %prior.3, f32[1]{0:T(128)S(6)} %copy.26.gate, bf16[1024,512]{1,0:T(8,128)(2,1)} %copy-done.2, ...), custom_call_target="tpu_custom_call" | custom-call | flops 10000000000 | bytes 20971520 | tf_op jit(solution)/shard_map/attend_and_finish/pallas_call | solution.py:367
  (11 shorter events, 0.1 us)
Async XLA Ops:
  0.0 51.0 %copy-start.9 = (s32[128]{0:T(128)S(1)}, s32[128]{0:T(128)}, u32[]{:S(2)}) copy-start(s32[128]{0:T(128)} %param.22) | copy-start | bytes 1540
  0.0 51.1 %copy-start = (bf16[128,512]{1,0:T(8,128)(2,1)S(1)}, bf16[128,512]{1,0:T(8,128)(2,1)}, u32[]{:S(2)}) copy-start(bf16[128,512]{1,0:T(8,128)(2,1)} %param.21) | copy-start | bytes 393220
  0.0 55.3 %copy-start.3 = (s32[4,2]{0,1:T(2,128)S(1)}, s32[4,2]{0,1:T(2,128)}, u32[]{:S(2)}) copy-start(s32[4,2]{0,1:T(2,128)} %param.36) | copy-start | bytes 100
  0.0 56.0 %copy-start.4 = (s32[4,2]{0,1:T(2,128)S(1)}, s32[4,2]{0,1:T(2,128)}, u32[]{:S(2)}) copy-start(s32[4,2]{0,1:T(2,128)} %param.37) | copy-start | bytes 100
  0.0 4.5 %collective-permute-start = (bf16[128,512]{1,0:T(8,128)(2,1)}, bf16[128,512]{1,0:T(8,128)(2,1)S(1)}, u32[]{:S(2)}, u32[]{:S(2)}) collective-permute-start(bf16[128,512]{1,0:T(8,128)(2,1)} %param.20), channel_id=1, source_target_pairs={{0,8},{8,0},{16,24},{24,16},{32,40},{40,32},{48,56},{56,48},{64,72... | collective-permute-start | bytes 393224 | tf_op jit(solution)/shard_map/ppermute | solution.py:42
  5.5 7.2 %collective-permute-start.1 = (bf16[256,512]{1,0:T(8,128)(2,1)S(1)}, bf16[256,512]{1,0:T(8,128)(2,1)S(1)}, u32[]{:S(2)}, u32[]{:S(2)}) collective-permute-start(bf16[256,512]{1,0:T(8,128)(2,1)S(1)} %pad_maximum_fusion.1), channel_id=1, source_target_pairs={{0,16},{8,120},{16,32},{24,8},{32,48},{40,24},{48,64},{56,40},{64,... | collective-permute-start | bytes 786440 | tf_op jit(solution)/shard_map/ppermute | solution.py:42
  12.7 6.4 %collective-permute-start.2 = (bf16[256,512]{1,0:T(8,128)(2,1)S(1)}, bf16[256,512]{1,0:T(8,128)(2,1)S(1)}, u32[]{:S(2)}, u32[]{:S(2)}) collective-permute-start(bf16[256,512]{1,0:T(8,128)(2,1)S(1)} %collective-permute-done.1), channel_id=1, source_target_pairs={{0,16},{8,120},{16,32},{24,8},{32,48},{40,24},{48,64},{56,40},{64,... | collective-permute-start | bytes 786440 | tf_op jit(solution)/shard_map/ppermute | solution.py:42
  19.1 6.4 %collective-permute-start.3 = (bf16[256,512]{1,0:T(8,128)(2,1)S(1)}, bf16[256,512]{1,0:T(8,128)(2,1)S(1)}, u32[]{:S(2)}, u32[]{:S(2)}) collective-permute-start(bf16[256,512]{1,0:T(8,128)(2,1)S(1)} %collective-permute-done.2), channel_id=1, source_target_pairs={{0,16},{8,120},{16,32},{24,8},{32,48},{40,24},{48,64},{56,40},{64,... | collective-permute-start | bytes 786440 | tf_op jit(solution)/shard_map/ppermute | solution.py:42
  25.6 5.1 %collective-permute-start.4 = (bf16[128,512]{1,0:T(8,128)(2,1)S(1)}, bf16[128,512]{1,0:T(8,128)(2,1)S(1)}, u32[]{:S(2)}, u32[]{:S(2)}) collective-permute-start(bf16[128,512]{1,0:T(8,128)(2,1)S(1)} %slice.4), channel_id=1, source_target_pairs={{0,16},{8,120},{16,32},{24,8},{32,48},{40,24},{48,64},{56,40},{64,... | collective-permute-start | bytes 393224 | tf_op jit(solution)/shard_map/ppermute | solution.py:42
  30.7 42.5 %copy-start.2 = (bf16[1024,512]{1,0:T(8,128)(2,1)}, bf16[1024,512]{1,0:T(8,128)(2,1)S(1)}, u32[]{:S(2)}) copy-start(bf16[1024,512]{1,0:T(8,128)(2,1)S(1)} %constant_dynamic-update-slice_fusion.part0) | copy-start | bytes 3145732
  30.7 14.9 %collective-permute-start.6 = (bf16[1024,512]{1,0:T(8,128)(2,1)S(1)}, bf16[1024,512]{1,0:T(8,128)(2,1)S(1)}, u32[]{:S(2)}, u32[]{:S(2)}) collective-permute-start(bf16[1024,512]{1,0:T(8,128)(2,1)S(1)} %constant_dynamic-update-slice_fusion.part0), channel_id=1, source_target_pairs={{0,129},{8,136},{16,145},{24,152},{32,161},{40,168},{48,177},{56,1... | collective-permute-start | bytes 3145736 | tf_op jit(solution)/shard_map/ppermute | solution.py:42
  32.0 45.5 %collective-permute-start.5 = (bf16[1024,512]{1,0:T(8,128)(2,1)S(1)}, bf16[1024,512]{1,0:T(8,128)(2,1)}, u32[]{:S(2)}, u32[]{:S(2)}) collective-permute-start(bf16[1024,512]{1,0:T(8,128)(2,1)S(1)} %constant_dynamic-update-slice_fusion.part0), channel_id=1, source_target_pairs={{0,8},{8,0},{16,24},{24,16},{32,40},{40,32},{48,56},{56,48},{64,72... | collective-permute-start | bytes 3145736 | tf_op jit(solution)/shard_map/ppermute | solution.py:42
  45.7 27.5 %copy-start.5 = (bf16[1024,512]{1,0:T(8,128)(2,1)}, bf16[1024,512]{1,0:T(8,128)(2,1)S(1)}, u32[]{:S(2)}) copy-start(bf16[1024,512]{1,0:T(8,128)(2,1)S(1)} %collective-permute-done.6.part2) | copy-start | bytes 3145732
  45.7 31.8 %collective-permute-start.7 = (bf16[1024,512]{1,0:T(8,128)(2,1)S(1)}, bf16[1024,512]{1,0:T(8,128)(2,1)}, u32[]{:S(2)}, u32[]{:S(2)}) collective-permute-start(bf16[1024,512]{1,0:T(8,128)(2,1)S(1)} %collective-permute-done.6.part2), channel_id=1, source_target_pairs={{0,8},{8,0},{16,24},{24,16},{32,40},{40,32},{48,56},{56,48},{64,72... | collective-permute-start | bytes 3145736 | tf_op jit(solution)/shard_map/ppermute | solution.py:42
  51.1 8.1 %collective-permute-start.8 = (bf16[128,640]{1,0:T(8,128)(2,1)S(1)}, bf16[128,640]{1,0:T(8,128)(2,1)S(1)}, u32[]{:S(2)}, u32[]{:S(2)}) collective-permute-start(bf16[128,640]{1,0:T(8,128)(2,1)S(1)} %pad_maximum_fusion.2), channel_id=1, source_target_pairs={{0,129},{8,137},{16,145},{24,153},{32,161},{40,169},{48,177},{56,1... | collective-permute-start | bytes 491528 | tf_op jit(solution)/shard_map/ppermute | solution.py:42
  59.2 14.0 %copy-start.1 = (bf16[256,640]{1,0:T(8,128)(2,1)}, bf16[256,640]{1,0:T(8,128)(2,1)S(1)}, u32[]{:S(2)}) copy-start(bf16[256,640]{1,0:T(8,128)(2,1)S(1)} %pad_maximum_fusion.ent0) | copy-start | bytes 983044
  59.2 14.0 %collective-permute-start.11 = (bf16[256,640]{1,0:T(8,128)(2,1)S(1)}, bf16[256,640]{1,0:T(8,128)(2,1)S(1)}, u32[]{:S(2)}, u32[]{:S(2)}) collective-permute-start(bf16[256,640]{1,0:T(8,128)(2,1)S(1)} %pad_maximum_fusion.ent0), channel_id=1, source_target_pairs={{0,4},{8,12},{16,20},{24,28},{32,36},{40,44},{48,52},{56,60},{64,6... | collective-permute-start | bytes 983048 | tf_op jit(solution)/shard_map/ppermute | solution.py:42
  62.2 15.2 %collective-permute-start.10 = (bf16[256,640]{1,0:T(8,128)(2,1)S(1)}, bf16[256,640]{1,0:T(8,128)(2,1)S(1)}, u32[]{:S(2)}, u32[]{:S(2)}) collective-permute-start(bf16[256,640]{1,0:T(8,128)(2,1)S(1)} %pad_maximum_fusion.ent0), channel_id=1, source_target_pairs={{0,2},{8,10},{16,18},{24,26},{32,34},{40,42},{48,50},{56,58},{64,6... | collective-permute-start | bytes 983048 | tf_op jit(solution)/shard_map/ppermute | solution.py:42
  62.6 14.9 %collective-permute-start.9 = (bf16[256,640]{1,0:T(8,128)(2,1)S(1)}, bf16[256,640]{1,0:T(8,128)(2,1)S(1)}, u32[]{:S(2)}, u32[]{:S(2)}) collective-permute-start(bf16[256,640]{1,0:T(8,128)(2,1)S(1)} %pad_maximum_fusion.ent0), channel_id=1, source_target_pairs={{0,6},{8,14},{16,22},{24,30},{32,38},{40,46},{48,54},{56,62},{64,7... | collective-permute-start | bytes 983048 | tf_op jit(solution)/shard_map/ppermute | solution.py:42
  73.2 4.3 %copy-start.6 = (bf16[256,640]{1,0:T(8,128)(2,1)}, bf16[256,640]{1,0:T(8,128)(2,1)S(1)}, u32[]{:S(2)}) copy-start(bf16[256,640]{1,0:T(8,128)(2,1)S(1)} %collective-permute-done.11.ent3) | copy-start | bytes 983044
  77.5 0.7 copy-start.7
  77.5 0.9 copy-start.8

commit v2 on v1

v2 whole, which is shorter than its diff:
```python
import functools
import math

import jax
import jax.numpy as jnp
from jax import lax
from jax.experimental import pallas as pl
from jax.experimental.pallas import tpu as pltpu
from jax.sharding import PartitionSpec as P

CAP = 20.0
D = 512
HEADS = 8
TILE = 128
PAIRS = 4
F32 = jnp.float32
BF16 = jnp.bfloat16
LOG2E = 1.4426950408889634
ZS, YS, XS = 8, 4, 4


def device_index(x, y, z, core):
    x_hi, x_lo = x // 2, x % 2
    return (x_lo * 16 + z * 2 + core) * 8 + (y * 2 + x_hi)


def permutation(move):
    pairs = []
    for x in range(XS):
        for y in range(YS):
            for z in range(ZS):
                for core in range(2):
                    tx, ty, tz, tc = move(x, y, z, core)
                    pairs.append(
                        (device_index(x, y, z, core), device_index(tx % XS, ty % YS, tz % ZS, tc))
                    )
    return pairs


def send(value, move):
    return lax.ppermute(value, ("paper", "type"), permutation(move))


def core_move(x, y, z, c):
    return (x, y, z, 1 - c)


def x_up(x, y, z, c):
    return (x - 1, y, z, c)


def x_down(x, y, z, c):
    return (x + 1, y, z, c)


def hi_move(x, y, z, c):
    return ({0: 3, 3: 0, 1: 2, 2: 1}[x], y, z, c)


def dot(a, b):
    return lax.dot_general(a, b, (((1,), (0,)), ((), ())), preferred_element_type=F32)


def dot_t(a, b):
    return lax.dot_general(a, b, (((1,), (1,)), ((), ())), preferred_element_type=F32)


def iota(shape, dim):
    return lax.broadcasted_iota(jnp.int32, shape, dim)


def low_half(rows):
    return (iota((rows, TILE), 1) & 64) == 0


def head_scale(prior, relation, j):
    return jnp.where(low_half(1), prior[relation, 2 * j], prior[relation, 2 * j + 1]) * (0.125 / CAP)


def mask_of(pattern, a, k, live):
    return jnp.where((pattern[a, k] > 0) & live, 1.0, 0.0).astype(BF16)


def fold_kernel(key_w, value_w, att, msg, cite_w, own_w, ent_w, blocks):
    lane = iota((64, 256), 1)
    row = iota((64, 256), 0)
    for i in range(4):
        place = (lane == row + 64 * i).astype(F32).astype(BF16)
        for t, rel in enumerate((att, msg)):
            for r in range(4):
                for g in range(2):
                    blocks[t, r, g, 64 * i : 64 * i + 64, :] = dot(rel[r, 4 * g + i], place).astype(
                        BF16
                    )
    for t, weight in enumerate((key_w, value_w)):
        for g in range(2):
            cols = slice(256 * g, 256 * g + 256)
            base = weight[0, :, cols]
            to = slice(512 * t + 256 * g, 512 * t + 256 * g + 256)
            cite_w[:, to] = dot(base, blocks[t, 0, g]).astype(BF16)
            own_w[:, to] = dot(base, blocks[t, 3, g]).astype(BF16)
            for u in range(2):
                ent_w[512 * u : 512 * u + 512, to] = dot(
                    weight[1 + u, :, cols], blocks[t, 1 + u, g]
                ).astype(BF16)


def own_kernel(papers, query_w, own_w, prior, q2, acc):
    half = low_half(1)
    zero = jnp.zeros((1, TILE), BF16)
    sums = ((iota((TILE, TILE), 0) & 64) == (iota((TILE, TILE), 1) & 64)).astype(F32).astype(BF16)
    rows = papers[...]
    for g in range(2):
        cols = slice(256 * g, 256 * g + 256)
        q_pairs = dot(rows, query_w[:, cols]).astype(BF16)
        k_pairs = dot(rows, own_w[:, cols]).astype(BF16)
        v_pairs = dot(rows, own_w[:, 512 + 256 * g : 512 + 256 * g + 256]).astype(BF16)
        for i in range(2):
            j = 2 * g + i
            part = slice(TILE * i, TILE * i + TILE)
            q, k, v = q_pairs[:, part], k_pairs[:, part], v_pairs[:, part]
            cols = slice(TILE * j, TILE * j + TILE)
            q2[0, :, cols] = jnp.where(half, q, zero)
            q2[1, :, cols] = jnp.where(half, zero, q)
            product = q.astype(F32) * k.astype(F32)
            high = product.astype(BF16)
            low = (product - high.astype(F32)).astype(BF16)
            score = dot(high, sums) + dot(low, sums)
            weight = jnp.exp2(jnp.tanh(score * head_scale(prior, 3, j)) * (CAP * LOG2E))
            den = pltpu.roll(weight, 64, 1)
            num = weight.astype(BF16).astype(F32) * v.astype(F32)
            acc[0, :, cols] = jnp.where(half, num, den)
            acc[1, :, cols] = jnp.where(half, den, num)


def source_kernel(part0, part1, part2, cite_w, pairs):
    base = 0
    for part in (part0, part1, part2):
        rows = part[...]
        at = slice(base, base + rows.shape[0])
        for n in range(4):
            pairs[at, 256 * n : 256 * n + 256] = dot(rows, cite_w[:, 256 * n : 256 * n + 256]).astype(
                BF16
            )
        base += rows.shape[0]


def entity_kernel(prior, ent0, ent1, ent_w, pairs, scales):
    type_at = lax.axis_index("type")
    y_at, hi_at = type_at // 2, type_at % 2
    pick = (iota((8, TILE), 1) == 0).astype(F32).astype(BF16)
    for s, part in enumerate((ent0, ent1)):
        rows = part[:, :D]
        kind = part[:, D : D + TILE]
        kind4 = jnp.concatenate([kind] * 4, axis=1)
        split = jnp.concatenate([rows * (1 - kind4), rows * kind4], axis=1)
        places = []
        for i in range(4):
            y = y_at if s == 0 else 3 - y_at
            y = y if i < 2 else y + 1 - 2 * (y % 2)
            places.append(y * 2 + (hi_at if i % 2 == 0 else 1 - hi_at))
        for n in range(4):
            made = dot(split, ent_w[:, 256 * n : 256 * n + 256]).astype(BF16)
            for t in range(4):
                at = pl.ds(pl.multiple_of(places[t] * TILE, TILE), TILE)
                pairs[at, 256 * n : 256 * n + 256] = made[TILE * t : TILE * t + TILE]
        for t in range(4):
            kind_row = dot_t(pick, kind[TILE * t : TILE * t + TILE])[0:1]
            for h in range(HEADS):
                scales[places[t], h : h + 1, :] = jnp.where(
                    kind_row < 0.5, prior[1, h], prior[2, h]
                ) * (0.125 / CAP)


def block_pair(q2, acc, rows, pairs, at0, at1, mask, scale_of):
    half = low_half(1)
    one = jnp.ones((1, TILE), BF16)
    at0 = pl.ds(pl.multiple_of(at0, TILE), TILE)
    at1 = pl.ds(pl.multiple_of(at1, TILE), TILE)
    for j in range(PAIRS):
        cols = slice(TILE * j, TILE * j + TILE)
        to = slice(D + TILE * j, D + TILE * j + TILE)
        kk = jnp.concatenate([pairs[at0, cols], pairs[at1, cols]], axis=0)
        vv = jnp.concatenate([pairs[at0, to], pairs[at1, to]], axis=0)
        for e in range(2):
            score = dot_t(q2[e, rows, cols], kk)
            weight = jnp.exp2(jnp.tanh(score * scale_of(2 * j + e)) * (CAP * LOG2E))
            value = jnp.where(half, vv, one) if e == 0 else jnp.where(half, one, vv)
            acc[e, rows, cols] += dot(weight.astype(BF16) * mask, value)


def final_kernel(
    tiles,
    counts,
    entity_tiles,
    entity_counts,
    prior,
    gate,
    near,
    near_other,
    far,
    far_other,
    entity_in,
    scales,
    q2_in,
    acc_in,
    pattern_in,
    entity_pattern_in,
    papers_in,
    output_w_in,
    gain,
    updated,
    pairs,
    entity_pairs,
    q2,
    acc,
    pattern,
    entity_pattern,
    papers,
    output_w,
    slots,
    sems,
):
    copies = []
    for source, target in (
        (q2_in, q2),
        (acc_in, acc),
        (entity_pattern_in, entity_pattern),
        (entity_in, entity_pairs),
        (near, pairs.at[pl.ds(0, 1024)]),
        (near_other, pairs.at[pl.ds(1024, 1024)]),
        (far, pairs.at[pl.ds(2048, 1024)]),
        (far_other, pairs.at[pl.ds(3072, 1024)]),
        (pattern_in, pattern),
        (output_w_in, output_w),
        (papers_in, papers),
    ):
        made = pltpu.make_async_copy(source, target, sems.at[len(copies)])
        made.start()
        copies.append(made)
    paper_at = lax.axis_index("paper")
    x_lo, z_at, core = paper_at // 16, (paper_at // 2) % ZS, paper_at % 2
    half = low_half(1)
    alpha = jax.nn.sigmoid(jnp.full((1, D), gate[0], F32))
    for made in copies:
        made.wait()

    def place(tile):
        far = jnp.where(tile // 16 == x_lo, 0, 2048)
        other = jnp.where(tile % 2 == core, 0, 1024)
        ahead = ((tile // 2) % ZS + ZS - z_at) % ZS
        at = jnp.where(ahead > 4, 2 * (ZS - ahead), jnp.maximum(2 * ahead - 1, 0))
        return far + other + at * TILE

    def tile_body(a, carry):
        rows = pl.ds(pl.multiple_of(a * TILE, TILE), TILE)
        e0, e1 = entity_tiles[a, 0], entity_tiles[a, 1]
        mask = jnp.concatenate(
            [mask_of(entity_pattern, a, k, entity_counts[a, k] > 0) for k in range(2)], axis=1
        )
        block_pair(
            q2,
            acc,
            rows,
            entity_pairs,
            e0 * TILE,
            e1 * TILE,
            mask,
            lambda h: jnp.concatenate([scales[e0, h : h + 1, :], scales[e1, h : h + 1, :]], axis=1),
        )
        count = jnp.int32(0)
        for k in range(8):
            slots[count] = k
            count = count + (counts[a, k] > 0).astype(jnp.int32)

        def pair_body(i, carry):
            k0 = slots[2 * i]
            second = 2 * i + 1 < count
            k1 = jnp.where(second, slots[2 * i + 1], k0)
            mask = jnp.concatenate(
                [mask_of(pattern, a, k0, True), mask_of(pattern, a, k1, second)], axis=1
            )
            block_pair(
                q2,
                acc,
                rows,
                pairs,
                place(tiles[a, k0]),
                place(tiles[a, k1]),
                mask,
                lambda h: prior[0, h] * (0.125 / CAP),
            )
            return carry

        lax.fori_loop(0, (count + 1) // 2, pair_body, 0)

        hidden = []
        for j in range(PAIRS):
            cols = slice(TILE * j, TILE * j + TILE)
            even, odd = acc[0, rows, cols], acc[1, rows, cols]
            num = jnp.where(half, even, odd)
            den = pltpu.roll(jnp.where(half, odd, even), 64, 1)
            mixed = num / den
            hidden.append((0.5 * mixed * (1.0 + lax.erf(mixed * math.sqrt(0.5)))).astype(BF16))
        projected = dot(jnp.concatenate(hidden, axis=1), output_w[...])
        blended = alpha * projected + (1.0 - alpha) * papers[rows, :].astype(F32)
        centre = jnp.mean(blended, axis=1, keepdims=True)
        blended = blended - centre
        spread = jnp.mean(jnp.square(blended), axis=1, keepdims=True)
        updated[rows, :] = (blended * lax.rsqrt(spread + 1e-05) * gain[...]).astype(BF16)
        return carry

    lax.fori_loop(0, 4, tile_body, 0)


def per_device(
    papers,
    cited_rows,
    entities,
    entity_kinds,
    query_weight,
    key_weight,
    value_weight,
    attention_rel,
    message_rel,
    relation_prior,
    output_weight,
    skip_gate,
    norm_gain,
    cite_pattern,
    cite_tiles,
    cite_counts,
    entity_pattern,
    entity_tiles,
    entity_counts,
):
    vmem = pl.BlockSpec(memory_space=pltpu.VMEM)
    smem = pl.BlockSpec(memory_space=pltpu.SMEM)
    shape = jax.ShapeDtypeStruct
    tie = lax.optimization_barrier

    def call(kernel, outs, ins, mib, flops, name, scratch=()):
        return pl.pallas_call(
            kernel,
            out_shape=outs,
            in_specs=ins,
            out_specs=jax.tree.map(lambda _: vmem, outs),
            scratch_shapes=scratch,
            compiler_params=pltpu.CompilerParams(vmem_limit_bytes=mib * 2**20),
            cost_estimate=pl.CostEstimate(
                flops=flops * 10**9, bytes_accessed=8 * 2**20, transcendentals=0
            ),
            name=name,
        )

    def up(value):
        return send(value, lambda x, y, z, c: (x, y, z + 1, c))

    def down(value):
        return send(value, lambda x, y, z, c: (x, y, z - 1, c))

    kinds = jnp.broadcast_to(entity_kinds.astype(BF16)[:, None], (TILE, TILE))
    ent_own = jnp.concatenate([entities, kinds], axis=1)
    a1, b1 = down(cited_rows), up(cited_rows)
    ent_x = send(ent_own, hi_move)
    a1, b1, ent_x = tie((a1, b1, ent_x))
    ent_pair = jnp.concatenate([ent_own, ent_x], axis=0)
    a2, b2 = down(a1), up(b1)
    ent_y = send(ent_pair, lambda x, y, z, c: (x, y ^ 1, z, c))
    a2, b2, ent_y = tie((a2, b2, ent_y))
    first = jnp.concatenate([cited_rows, a1, b1, a2], axis=0)
    ent_four = jnp.concatenate([ent_pair, ent_y], axis=0)
    a3, b3 = down(a2), up(b2)
    far_first = send(first, x_up)
    ent_rest = send(ent_four, lambda x, y, z, c: (x, 3 - y, z, c))
    cite_w, own_w, ent_w = call(
        fold_kernel,
        (shape((D, 2 * D), BF16), shape((D, 2 * D), BF16), shape((2 * D, 2 * D), BF16)),
        [vmem] * 4,
        20,
        3,
        "fold_maps",
        [pltpu.VMEM((2, 4, 2, 256, 256), BF16)],
    )(key_weight, value_weight, attention_rel, message_rel)
    a3, b3, cite_w = tie((a3, b3, cite_w))
    a4 = down(a3)
    second = jnp.concatenate([b2, a3], axis=0)
    far_second = send(second, x_up)
    a4, second = tie((a4, second))
    third = jnp.concatenate([b3, a4], axis=0)
    far_third = send(third, x_down)
    source = call(source_kernel, shape((1024, 2 * D), BF16), [vmem] * 4, 16, 2, "cited_sources")
    near = source(first, second, third, cite_w)
    near_other = send(near, core_move)
    entity_pairs, scales = call(
        entity_kernel,
        (shape((1024, 2 * D), BF16), shape((8, HEADS, TILE), F32)),
        [smem] + [vmem] * 3,
        20,
        2,
        "entity_sources",
    )(relation_prior, ent_four, ent_rest, ent_w)
    far_first, far_second, far_third, entity_pairs = tie(
        (far_first, far_second, far_third, entity_pairs)
    )
    far = source(far_first, far_second, far_third, cite_w)
    far_other = send(far, core_move)
    far, own_w = tie((far, own_w))
    q2, acc = call(
        own_kernel,
        (shape((2, 512, D), BF16), shape((2, 512, D), F32)),
        [vmem] * 3 + [smem],
        16,
        1,
        "own_terms",
    )(papers, query_weight, own_w, relation_prior)

    hbm = pl.BlockSpec(memory_space=pl.ANY)
    return call(
        final_kernel,
        shape((512, D), BF16),
        [smem] * 6 + [hbm] * 5 + [vmem] + [hbm] * 6 + [vmem],
        26,
        4,
        "attend_and_finish",
        [
            pltpu.VMEM((4096, 2 * D), BF16),
            pltpu.VMEM((1024, 2 * D), BF16),
            pltpu.VMEM((2, 512, D), BF16),
            pltpu.VMEM((2, 512, D), F32),
            pltpu.VMEM((4, 8, TILE, TILE), jnp.int32),
            pltpu.VMEM((4, 2, TILE, TILE), jnp.int32),
            pltpu.VMEM((512, D), BF16),
            pltpu.VMEM((D, D), BF16),
            pltpu.SMEM((16,), jnp.int32),
            pltpu.SemaphoreType.DMA((11,)),
        ],
    )(
        cite_tiles,
        cite_counts,
        entity_tiles,
        entity_counts,
        relation_prior,
        skip_gate,
        near,
        near_other,
        far,
        far_other,
        entity_pairs,
        scales,
        q2,
        acc,
        cite_pattern,
        entity_pattern,
        papers,
        output_weight,
        norm_gain.reshape(1, D),
    )


def solution(mesh):
    split = P(("paper", "type"))
    in_specs = (
        P(("paper", "type"), None),
        P("paper", None),
        P("type", None),
        P("type"),
        P(),
        P(),
        P(),
        P(),
        P(),
        P(),
        P(),
        P(),
        P(),
        split,
        split,
        split,
        split,
        split,
        split,
    )
    return jax.shard_map(
        per_device, mesh=mesh, in_specs=in_specs, out_specs=P(("paper", "type"), None), check_vma=False
    )
```

time: 109 us -> 80.4 us (0.74)
  the two profiles are of different devices: /device:TPU:1 before, /device:TPU:9 now
where the time goes in v2:
time: 80.4 us; the launch traced here: 79 us
  Pallas kernels  32.4 us (40%)
  starting transfers between devices  23.4 us (29%)
  waiting for transfers between devices  12.2 us (15%)
  local copies, waits for them, and re-layouts  8.12 us (10%)
  other arithmetic  1.67 us (2%)
  between operations  1.16 us (1%)
    ppermute x15, starting transfers between devices, send(): return lax.ppermute(value, ('paper', 'type'), permutation(move))  23.4 us
    pallas_call x1, Pallas kernels, per_device(): call(final_kernel, shape((512, D), BF16), [smem] * 6 + [hbm] * 5 + [vmem]...  21.6 us
    ppermute x15, waiting for transfers between devices, send(): return lax.ppermute(value, ('paper', 'type'), permutation(move))  12.2 us
    unnamed x49, local copies, waits for them, and re-layouts  8.01 us
    pallas_call x1, Pallas kernels, per_device(): call(entity_kernel, (shape((1024, 2 * D), BF16), shape((8, HEADS, TILE),...  3.21 us
    pallas_call x1, Pallas kernels, per_device(): far = source(far_first, far_second, far_third, cite_w)  2.59 us
    pallas_call x1, Pallas kernels, per_device(): call(own_kernel, (shape((2, 512, D), BF16), shape((2, 512, D), F32)), [vm...  2.06 us
    pallas_call x1, Pallas kernels, per_device(): call(fold_kernel, (shape((D, 2 * D), BF16), shape((D, 2 * D), BF16), shap...  1.71 us
  transfers between devices with their start and end apart: 15, of which 5 were waited for; matrix products, arithmetic and copies ran while one was open for 3% of the time, Pallas kernels for 14%

profile of v2, /device:TPU:9, one launch (start us, length us, event | category | flops | bytes accessed | tf_op | source)
XLA Modules:
  0.0 79.0 jit_solution(24546317253968600)
XLA Ops:
  0.0 5.6 %collective-permute-start = (bf16[128,512]{1,0:T(8,128)(2,1)}, bf16[128,512]{1,0:T(8,128)(2,1)S(1)}, u32[]{:S(2)}, u32[]{:S(2)}) collective-permute-start(bf16[128,512]{1,0:T(8,128)(2,1)} %param.20), channel_id=1, source_target_pairs={{0,112},{8,120},{16,0},{24,8},{32,16},{40,24},{48,32},{56,40},{64,... | collective-permute-start | bytes 393224 | tf_op jit(solution)/shard_map/ppermute | solution.py:41
  5.6 0.0 collective-permute-start.1
  5.6 0.7 convert_element_type.3
  6.2 0.1 broadcast_in_dim.2
  6.3 0.9 %pad_maximum_fusion.2 = bf16[128,640]{1,0:T(8,128)(2,1)S(1)} fusion(bf16[128,128]{1,0:T(8,128)(2,1)S(1)} %broadcast_in_dim.2, bf16[128,512]{1,0:T(8,128)(2,1)} %param.21), kind=kLoop, calls=%fused_computation.2 | loop fusion | flops 327680 | bytes 327680 | tf_op jit(solution)/shard_map/concatenate | solution.py:363
  7.3 2.6 %collective-permute-start.2 = (bf16[128,640]{1,0:T(8,128)(2,1)S(1)}, bf16[128,640]{1,0:T(8,128)(2,1)S(1)}, u32[]{:S(2)}, u32[]{:S(2)}) collective-permute-start(bf16[128,640]{1,0:T(8,128)(2,1)S(1)} %pad_maximum_fusion.2), channel_id=1, source_target_pairs={{0,129},{8,137},{16,145},{24,153},{32,161},{40,169},{48,177},{56,1... | collective-permute-start | bytes 491528 | tf_op jit(solution)/shard_map/ppermute | solution.py:41
  9.8 1.4 %copy-done.10 = bf16[3,512,512]{2,1,0:T(8,128)(2,1)S(1)} copy-done((bf16[3,512,512]{2,1,0:T(8,128)(2,1)S(1)}, bf16[3,512,512]{2,1,0:T(8,128)(2,1)}, u32[]{:S(2)}) %copy-start.10) | copy-done | bytes 1572888
  11.2 1.4 %copy-done.11 = bf16[3,512,512]{2,1,0:T(8,128)(2,1)S(1)} copy-done((bf16[3,512,512]{2,1,0:T(8,128)(2,1)S(1)}, bf16[3,512,512]{2,1,0:T(8,128)(2,1)}, u32[]{:S(2)}) %copy-start.11) | copy-done | bytes 1572888
  12.6 1.0 %copy-done.12 = bf16[4,8,64,64]{3,2,1,0:T(8,128)(2,1)S(1)} copy-done((bf16[4,8,64,64]{3,2,1,0:T(8,128)(2,1)S(1)}, bf16[4,8,64,64]{3,2,1,0:T(8,128)(2,1)}, u32[]{:S(2)}) %copy-start.12) | copy-done | bytes 262168
  13.7 1.0 %copy-done.13 = bf16[4,8,64,64]{3,2,1,0:T(8,128)(2,1)S(1)} copy-done((bf16[4,8,64,64]{3,2,1,0:T(8,128)(2,1)S(1)}, bf16[4,8,64,64]{3,2,1,0:T(8,128)(2,1)}, u32[]{:S(2)}) %copy-start.13) | copy-done | bytes 262168
  14.7 1.7 %fold_maps.1 = (bf16[512,1024]{1,0:T(8,128)(2,1)S(1)}, bf16[512,1024]{1,0:T(8,128)(2,1)S(1)}, bf16[1024,1024]{1,0:T(8,128)(2,1)S(1)}) custom-call(bf16[3,512,512]{2,1,0:T(8,128)(2,1)S(1)} %copy-done.10, bf16[3,512,512]{2,1,0:T(8,128)(2,1)S(1)} %copy-done.11, bf16[4,8,64,64]{3,2,1,0:T(8,128)(2,1)S(1)} %copy-done.12, bf16[4,8,64,64]{3,2,1,0:T(8,128)(2,1)S(1)} %copy-done.13), custom_call_target="tpu_custom_call" | custom-call | flops 3000000000 | bytes 8388608 | tf_op jit(solution)/shard_map/fold_maps/pallas_call | solution.py:376
  16.5 0.0 collective-permute-done.2
  16.5 0.2 collective-permute-start.5
  16.8 2.7 %collective-permute-start.3 = (bf16[128,512]{1,0:T(8,128)(2,1)S(1)}, bf16[128,512]{1,0:T(8,128)(2,1)S(1)}, u32[]{:S(2)}, u32[]{:S(2)}) collective-permute-start(bf16[128,512]{1,0:T(8,128)(2,1)S(1)} %collective-permute-done), channel_id=1, source_target_pairs={{0,112},{8,120},{16,0},{24,8},{32,16},{40,24},{48,32},{56,40},{64,... | collective-permute-start | bytes 393224 | tf_op jit(solution)/shard_map/ppermute | solution.py:41
  19.5 0.0 collective-permute-start.4
  19.6 1.9 %collective-permute-done.3 = bf16[128,512]{1,0:T(8,128)(2,1)S(1)} collective-permute-done((bf16[128,512]{1,0:T(8,128)(2,1)S(1)}, bf16[128,512]{1,0:T(8,128)(2,1)S(1)}, u32[]{:S(2)}, u32[]{:S(2)}) %collective-permute-start.3) | collective-permute-done | bytes 131104 | tf_op jit(solution)/shard_map/ppermute | solution.py:41
  21.5 3.1 %collective-permute-done.4 = bf16[128,512]{1,0:T(8,128)(2,1)S(1)} collective-permute-done((bf16[128,512]{1,0:T(8,128)(2,1)S(1)}, bf16[128,512]{1,0:T(8,128)(2,1)S(1)}, u32[]{:S(2)}, u32[]{:S(2)}) %collective-permute-start.4) | collective-permute-done | bytes 131104 | tf_op jit(solution)/shard_map/ppermute | solution.py:41
  24.6 0.0 collective-permute-done.5
  24.6 2.4 %collective-permute-start.6 = (bf16[128,512]{1,0:T(8,128)(2,1)S(1)}, bf16[128,512]{1,0:T(8,128)(2,1)S(1)}, u32[]{:S(2)}, u32[]{:S(2)}) collective-permute-start(bf16[128,512]{1,0:T(8,128)(2,1)S(1)} %collective-permute-done.3), channel_id=1, source_target_pairs={{0,112},{8,120},{16,0},{24,8},{32,16},{40,24},{48,32},{56,40},{64,... | collective-permute-start | bytes 393224 | tf_op jit(solution)/shard_map/ppermute | solution.py:41
  27.0 0.0 collective-permute-start.7
  27.0 0.1 pad_maximum_fusion.ent0
  27.1 1.4 %collective-permute-start.13 = (bf16[512,640]{1,0:T(8,128)(2,1)S(1)}, bf16[512,640]{1,0:T(8,128)(2,1)S(1)}, u32[]{:S(2)}, u32[]{:S(2)}) collective-permute-start(bf16[512,640]{1,0:T(8,128)(2,1)S(1)} %pad_maximum_fusion.ent0), channel_id=1, source_target_pairs={{0,6},{8,14},{16,22},{24,30},{32,38},{40,46},{48,54},{56,62},{64,7... | collective-permute-start | bytes 1966088 | tf_op jit(solution)/shard_map/ppermute | solution.py:41
  28.4 0.3 collective-permute-start.10
  28.7 0.2 collective-permute-done.6
  28.9 3.1 %collective-permute-done.7 = bf16[128,512]{1,0:T(8,128)(2,1)S(1)} collective-permute-done((bf16[128,512]{1,0:T(8,128)(2,1)S(1)}, bf16[128,512]{1,0:T(8,128)(2,1)S(1)}, u32[]{:S(2)}, u32[]{:S(2)}) %collective-permute-start.7) | collective-permute-done | bytes 131104 | tf_op jit(solution)/shard_map/ppermute | solution.py:41
  32.1 0.2 collective-permute-start.11
  32.3 3.8 %collective-permute-done.8 = bf16[128,512]{1,0:T(8,128)(2,1)S(1)} collective-permute-done((bf16[128,512]{1,0:T(8,128)(2,1)S(1)}, bf16[128,512]{1,0:T(8,128)(2,1)S(1)}, u32[]{:S(2)}, u32[]{:S(2)}) %collective-permute-start.8) | collective-permute-done | bytes 131104 | tf_op jit(solution)/shard_map/ppermute | solution.py:41
  36.1 0.0 copy-start.8
  36.2 0.3 collective-permute-start.12
  36.4 1.3 %cited_sources.2.near = bf16[1024,1024]{1,0:T(8,128)(2,1)S(1)} custom-call(bf16[512,512]{1,0:T(8,128)(2,1)S(1)} %constant_dynamic-update-slice_fusion.part0, bf16[256,512]{1,0:T(8,128)(2,1)S(1)} %constant_dynamic-update-slice_fusion.4.part1, bf16[256,512]{1,0:T(8,128)(2,1)S(1)} %constant_dynamic-update-slice_fusion.6.part2, ...), custom_call_target="tpu_custom_call" | custom-call | flops 2000000000 | bytes 8388608 | tf_op jit(solution)/shard_map/cited_sources/pallas_call | solution.py:393
  37.7 5.0 %collective-permute-start.9 = (bf16[1024,1024]{1,0:T(8,128)(2,1)S(1)}, bf16[1024,1024]{1,0:T(8,128)(2,1)}, u32[]{:S(2)}, u32[]{:S(2)}) collective-permute-start(bf16[1024,1024]{1,0:T(8,128)(2,1)S(1)} %cited_sources.2.near), channel_id=1, source_target_pairs={{0,8},{8,0},{16,24},{24,16},{32,40},{40,32},{48,56},{56,48},{64,72... | collective-permute-start | bytes 6291464 | tf_op jit(solution)/shard_map/ppermute | solution.py:41
  42.7 0.0 collective-permute-done.13.ent1
  42.7 3.2 %entity_sources.1 = (bf16[1024,1024]{1,0:T(8,128)(2,1)S(1)}, f32[8,8,128]{2,1,0:T(8,128)S(1)}) custom-call(f32[4,8]{1,0:T(4,128)S(1)} %copy-done.8, bf16[512,640]{1,0:T(8,128)(2,1)S(1)} %pad_maximum_fusion.ent0, bf16[512,640]{1,0:T(8,128)(2,1)S(1)} %collective-permute-done.13.ent1, bf16[1024,1024]{1,0:T(8,128)(2,1)S(1)} %get-tuple-element.41.ent_w), custom_call_target="tpu_custom_call" | custom-call | flops 2000000000 | bytes 8388608 | tf_op jit(solution)/shard_map/entity_sources/pallas_call | solution.py:395
  46.0 0.0 collective-permute-done.12.part2
  46.0 0.0 copy-start.19
  46.0 0.0 copy-start.20
  46.0 0.0 copy-start.3
  46.0 0.0 copy-start.14
  46.0 2.6 %cited_sources.3.far = bf16[1024,1024]{1,0:T(8,128)(2,1)} custom-call(bf16[512,512]{1,0:T(8,128)(2,1)S(1)} %collective-permute-done.10.part0, bf16[256,512]{1,0:T(8,128)(2,1)S(1)} %collective-permute-done.11.part1, bf16[256,512]{1,0:T(8,128)(2,1)S(1)} %collective-permute-done.12.part2, bf16[512,1024]{1,0:T(8,128)(2,1)S(1)} %get-tuple-element.39.cite_w), custom_call_target="tpu_custom_call" | custom-call | flops 2000000000 | bytes 8388608 | tf_op jit(solution)/shard_map/cited_sources/pallas_call | solution.py:406
  48.6 2.7 %collective-permute-start.14 = (bf16[1024,1024]{1,0:T(8,128)(2,1)}, bf16[1024,1024]{1,0:T(8,128)(2,1)}, u32[]{:S(2)}, u32[]{:S(2)}) collective-permute-start(bf16[1024,1024]{1,0:T(8,128)(2,1)} %cited_sources.3.far), channel_id=1, source_target_pairs={{0,8},{8,0},{16,24},{24,16},{32,40},{40,32},{48,56},{56,48},{64,72... | collective-permute-start | bytes 6291464 | tf_op jit(solution)/shard_map/ppermute | solution.py:41
  51.3 0.1 copy.20.entity_tiles
  51.4 0.1 copy.21.entity_counts
  52.2 1.2 %copy-done.16 = bf16[512,1024]{1,0:T(8,128)(2,1)S(1)} copy-done((bf16[512,1024]{1,0:T(8,128)(2,1)S(1)}, bf16[512,1024]{1,0:T(8,128)(2,1)}, u32[]{:S(2)}) %copy-start.16) | copy-done | bytes 1048600
  53.4 0.0 copy-start.7
  53.4 0.0 copy-start.9
  53.5 2.1 %own_terms.1 = (bf16[2,512,512]{2,1,0:T(8,128)(2,1)S(1)}, f32[2,512,512]{2,1,0:T(8,128)S(1)}) custom-call(bf16[512,512]{1,0:T(8,128)(2,1)S(1)} %copy-done.3, bf16[512,512]{1,0:T(8,128)(2,1)S(1)} %copy-done.14, bf16[512,1024]{1,0:T(8,128)(2,1)S(1)} %copy-done.16, f32[4,8]{1,0:T(4,128)S(1)} %copy-done.8), custom_call_target="tpu_custom_call" | custom-call | flops 1000000000 | bytes 8388608 | tf_op jit(solution)/shard_map/own_terms/pallas_call | solution.py:409
  55.6 1.6 %copy-done.2 = bf16[1024,1024]{1,0:T(8,128)(2,1)S(1)} copy-done((bf16[1024,1024]{1,0:T(8,128)(2,1)S(1)}, bf16[1024,1024]{1,0:T(8,128)(2,1)}, u32[]{:S(2)}) %copy-start.2) | copy-done | bytes 2097176
  57.2 21.6 %attend_and_finish.1 = bf16[512,512]{1,0:T(8,128)(2,1)} custom-call(s32[4,8]{1,0:T(4,128)S(1)} %copy-done.6, s32[4,8]{1,0:T(4,128)S(1)} %copy-done.7, s32[4,2]{1,0:T(4,128)S(1)} %copy.20.entity_tiles, s32[4,2]{1,0:T(4,128)S(1)} %copy.21.entity_counts, f32[4,8]{1,0:T(4,128)S(1)} %copy-done.8, f32[1]{0:T(128)S(6)} %copy.27.gate, ...), custom_call_target="tpu_custom_call" | custom-call | flops 4000000000 | bytes 8388608 | tf_op jit(solution)/shard_map/attend_and_finish/pallas_call | solution.py:419
  (45 shorter events, 0.2 us)
Async XLA Ops:
  0.0 16.5 %collective-permute-start = (bf16[128,512]{1,0:T(8,128)(2,1)}, bf16[128,512]{1,0:T(8,128)(2,1)S(1)}, u32[]{:S(2)}, u32[]{:S(2)}) collective-permute-start(bf16[128,512]{1,0:T(8,128)(2,1)} %param.20), channel_id=1, source_target_pairs={{0,112},{8,120},{16,0},{24,8},{32,16},{40,24},{48,32},{56,40},{64,... | collective-permute-start | bytes 393224 | tf_op jit(solution)/shard_map/ppermute | solution.py:41
  5.6 10.9 %collective-permute-start.1 = (bf16[128,512]{1,0:T(8,128)(2,1)}, bf16[128,512]{1,0:T(8,128)(2,1)S(1)}, u32[]{:S(2)}, u32[]{:S(2)}) collective-permute-start(bf16[128,512]{1,0:T(8,128)(2,1)} %param.20), channel_id=1, source_target_pairs={{0,16},{8,24},{16,32},{24,40},{32,48},{40,56},{48,64},{56,72},{64,... | collective-permute-start | bytes 393224 | tf_op jit(solution)/shard_map/ppermute | solution.py:41
  7.3 9.2 %collective-permute-start.2 = (bf16[128,640]{1,0:T(8,128)(2,1)S(1)}, bf16[128,640]{1,0:T(8,128)(2,1)S(1)}, u32[]{:S(2)}, u32[]{:S(2)}) collective-permute-start(bf16[128,640]{1,0:T(8,128)(2,1)S(1)} %pad_maximum_fusion.2), channel_id=1, source_target_pairs={{0,129},{8,137},{16,145},{24,153},{32,161},{40,169},{48,177},{56,1... | collective-permute-start | bytes 491528 | tf_op jit(solution)/shard_map/ppermute | solution.py:41
  9.8 1.4 %copy-start.10 = (bf16[3,512,512]{2,1,0:T(8,128)(2,1)S(1)}, bf16[3,512,512]{2,1,0:T(8,128)(2,1)}, u32[]{:S(2)}) copy-start(bf16[3,512,512]{2,1,0:T(8,128)(2,1)} %key_w.1) | copy-start | bytes 4718596
  11.2 1.4 %copy-start.11 = (bf16[3,512,512]{2,1,0:T(8,128)(2,1)S(1)}, bf16[3,512,512]{2,1,0:T(8,128)(2,1)}, u32[]{:S(2)}) copy-start(bf16[3,512,512]{2,1,0:T(8,128)(2,1)} %value_w.1) | copy-start | bytes 4718596
  12.6 1.0 %copy-start.12 = (bf16[4,8,64,64]{3,2,1,0:T(8,128)(2,1)S(1)}, bf16[4,8,64,64]{3,2,1,0:T(8,128)(2,1)}, u32[]{:S(2)}) copy-start(bf16[4,8,64,64]{3,2,1,0:T(8,128)(2,1)} %att.1) | copy-start | bytes 786436
  13.7 1.0 %copy-start.13 = (bf16[4,8,64,64]{3,2,1,0:T(8,128)(2,1)S(1)}, bf16[4,8,64,64]{3,2,1,0:T(8,128)(2,1)}, u32[]{:S(2)}) copy-start(bf16[4,8,64,64]{3,2,1,0:T(8,128)(2,1)} %msg.1) | copy-start | bytes 786436
  14.7 1.8 %copy-start.17 = (bf16[128,512]{1,0:T(8,128)(2,1)S(1)}, bf16[128,512]{1,0:T(8,128)(2,1)}, u32[]{:S(2)}) copy-start(bf16[128,512]{1,0:T(8,128)(2,1)} %param.21) | copy-start | bytes 393220
  14.7 2.1 %copy-start.18 = (bf16[128,512]{1,0:T(8,128)(2,1)S(1)}, bf16[128,512]{1,0:T(8,128)(2,1)}, u32[]{:S(2)}) copy-start(bf16[128,512]{1,0:T(8,128)(2,1)} %param.20) | copy-start | bytes 393220
  16.4 10.5 %copy-start.15 = (bf16[512,1024]{1,0:T(8,128)(2,1)}, bf16[512,1024]{1,0:T(8,128)(2,1)S(1)}, u32[]{:S(2)}) copy-start(bf16[512,1024]{1,0:T(8,128)(2,1)S(1)} %get-tuple-element.50.own_w) | copy-start | bytes 3145732
  16.5 8.1 %collective-permute-start.5 = (bf16[256,640]{1,0:T(8,128)(2,1)S(1)}, bf16[256,640]{1,0:T(8,128)(2,1)S(1)}, u32[]{:S(2)}, u32[]{:S(2)}) collective-permute-start(bf16[256,640]{1,0:T(8,128)(2,1)S(1)} %pad_maximum_fusion.1), channel_id=1, source_target_pairs={{0,2},{8,10},{16,18},{24,26},{32,34},{40,42},{48,50},{56,58},{64,6... | collective-permute-start | bytes 983048 | tf_op jit(solution)/shard_map/ppermute | solution.py:41
  16.8 4.7 %collective-permute-start.3 = (bf16[128,512]{1,0:T(8,128)(2,1)S(1)}, bf16[128,512]{1,0:T(8,128)(2,1)S(1)}, u32[]{:S(2)}, u32[]{:S(2)}) collective-permute-start(bf16[128,512]{1,0:T(8,128)(2,1)S(1)} %collective-permute-done), channel_id=1, source_target_pairs={{0,112},{8,120},{16,0},{24,8},{32,16},{40,24},{48,32},{56,40},{64,... | collective-permute-start | bytes 393224 | tf_op jit(solution)/shard_map/ppermute | solution.py:41
  19.5 5.0 %collective-permute-start.4 = (bf16[128,512]{1,0:T(8,128)(2,1)S(1)}, bf16[128,512]{1,0:T(8,128)(2,1)S(1)}, u32[]{:S(2)}, u32[]{:S(2)}) collective-permute-start(bf16[128,512]{1,0:T(8,128)(2,1)S(1)} %collective-permute-done.1), channel_id=1, source_target_pairs={{0,16},{8,24},{16,32},{24,40},{32,48},{40,56},{48,64},{56,72},{64,... | collective-permute-start | bytes 393224 | tf_op jit(solution)/shard_map/ppermute | solution.py:41
  24.6 4.3 %collective-permute-start.6 = (bf16[128,512]{1,0:T(8,128)(2,1)S(1)}, bf16[128,512]{1,0:T(8,128)(2,1)S(1)}, u32[]{:S(2)}, u32[]{:S(2)}) collective-permute-start(bf16[128,512]{1,0:T(8,128)(2,1)S(1)} %collective-permute-done.3), channel_id=1, source_target_pairs={{0,112},{8,120},{16,0},{24,8},{32,16},{40,24},{48,32},{56,40},{64,... | collective-permute-start | bytes 393224 | tf_op jit(solution)/shard_map/ppermute | solution.py:41
  27.0 5.0 %collective-permute-start.7 = (bf16[128,512]{1,0:T(8,128)(2,1)S(1)}, bf16[128,512]{1,0:T(8,128)(2,1)S(1)}, u32[]{:S(2)}, u32[]{:S(2)}) collective-permute-start(bf16[128,512]{1,0:T(8,128)(2,1)S(1)} %collective-permute-done.4), channel_id=1, source_target_pairs={{0,16},{8,24},{16,32},{24,40},{32,48},{40,56},{48,64},{56,72},{64,... | collective-permute-start | bytes 393224 | tf_op jit(solution)/shard_map/ppermute | solution.py:41
  27.1 15.7 %collective-permute-start.13 = (bf16[512,640]{1,0:T(8,128)(2,1)S(1)}, bf16[512,640]{1,0:T(8,128)(2,1)S(1)}, u32[]{:S(2)}, u32[]{:S(2)}) collective-permute-start(bf16[512,640]{1,0:T(8,128)(2,1)S(1)} %pad_maximum_fusion.ent0), channel_id=1, source_target_pairs={{0,6},{8,14},{16,22},{24,30},{32,38},{40,46},{48,54},{56,62},{64,7... | collective-permute-start | bytes 1966088 | tf_op jit(solution)/shard_map/ppermute | solution.py:41
  28.4 17.5 %collective-permute-start.10 = (bf16[512,512]{1,0:T(8,128)(2,1)S(1)}, bf16[512,512]{1,0:T(8,128)(2,1)S(1)}, u32[]{:S(2)}, u32[]{:S(2)}) collective-permute-start(bf16[512,512]{1,0:T(8,128)(2,1)S(1)} %constant_dynamic-update-slice_fusion.part0), channel_id=1, source_target_pairs={{0,129},{8,137},{16,145},{24,153},{32,161},{40,169},{48,177},{56,1... | collective-permute-start | bytes 1572872 | tf_op jit(solution)/shard_map/ppermute | solution.py:41
  32.0 4.1 %collective-permute-start.8 = (bf16[128,512]{1,0:T(8,128)(2,1)S(1)}, bf16[128,512]{1,0:T(8,128)(2,1)S(1)}, u32[]{:S(2)}, u32[]{:S(2)}) collective-permute-start(bf16[128,512]{1,0:T(8,128)(2,1)S(1)} %collective-permute-done.6), channel_id=1, source_target_pairs={{0,112},{8,120},{16,0},{24,8},{32,16},{40,24},{48,32},{56,40},{64,... | collective-permute-start | bytes 393224 | tf_op jit(solution)/shard_map/ppermute | solution.py:41
  32.1 13.9 %collective-permute-start.11 = (bf16[256,512]{1,0:T(8,128)(2,1)S(1)}, bf16[256,512]{1,0:T(8,128)(2,1)S(1)}, u32[]{:S(2)}, u32[]{:S(2)}) collective-permute-start(bf16[256,512]{1,0:T(8,128)(2,1)S(1)} %constant_dynamic-update-slice_fusion.4.part1), channel_id=1, source_target_pairs={{0,129},{8,137},{16,145},{24,153},{32,161},{40,169},{48,177},{56,1... | collective-permute-start | bytes 786440 | tf_op jit(solution)/shard_map/ppermute | solution.py:41
  36.1 6.6 %copy-start.8 = (f32[4,8]{1,0:T(4,128)S(1)}, f32[4,8]{1,0:T(4,128)}, u32[]{:S(2)}) copy-start(f32[4,8]{1,0:T(4,128)} %prior.5) | copy-start | bytes 388
  36.2 9.8 %collective-permute-start.12 = (bf16[256,512]{1,0:T(8,128)(2,1)S(1)}, bf16[256,512]{1,0:T(8,128)(2,1)S(1)}, u32[]{:S(2)}, u32[]{:S(2)}) collective-permute-start(bf16[256,512]{1,0:T(8,128)(2,1)S(1)} %constant_dynamic-update-slice_fusion.6.part2), channel_id=1, source_target_pairs={{0,128},{8,136},{16,144},{24,152},{32,160},{40,168},{48,176},{56,1... | collective-permute-start | bytes 786440 | tf_op jit(solution)/shard_map/ppermute | solution.py:41
  37.7 17.8 %collective-permute-start.9 = (bf16[1024,1024]{1,0:T(8,128)(2,1)S(1)}, bf16[1024,1024]{1,0:T(8,128)(2,1)}, u32[]{:S(2)}, u32[]{:S(2)}) collective-permute-start(bf16[1024,1024]{1,0:T(8,128)(2,1)S(1)} %cited_sources.2.near), channel_id=1, source_target_pairs={{0,8},{8,0},{16,24},{24,16},{32,40},{40,32},{48,56},{56,48},{64,72... | collective-permute-start | bytes 6291464 | tf_op jit(solution)/shard_map/ppermute | solution.py:41
  45.9 2.7 %copy-start.1 = (bf16[1024,1024]{1,0:T(8,128)(2,1)}, bf16[1024,1024]{1,0:T(8,128)(2,1)S(1)}, u32[]{:S(2)}) copy-start(bf16[1024,1024]{1,0:T(8,128)(2,1)S(1)} %get-tuple-element.48.entity_in) | copy-start | bytes 6291460
  46.0 5.4 %copy-start.19 = (s32[4,2]{0,1:T(2,128)S(1)}, s32[4,2]{0,1:T(2,128)}, u32[]{:S(2)}) copy-start(s32[4,2]{0,1:T(2,128)} %param.36) | copy-start | bytes 100
  46.0 5.4 %copy-start.20 = (s32[4,2]{0,1:T(2,128)S(1)}, s32[4,2]{0,1:T(2,128)}, u32[]{:S(2)}) copy-start(s32[4,2]{0,1:T(2,128)} %param.37) | copy-start | bytes 100
  46.0 6.2 %copy-start.3 = (bf16[512,512]{1,0:T(8,128)(2,1)S(1)}, bf16[512,512]{1,0:T(8,128)(2,1)}, u32[]{:S(2)}) copy-start(bf16[512,512]{1,0:T(8,128)(2,1)} %papers_in.1) | copy-start | bytes 1572868
  46.0 6.2 %copy-start.14 = (bf16[512,512]{1,0:T(8,128)(2,1)S(1)}, bf16[512,512]{1,0:T(8,128)(2,1)}, u32[]{:S(2)}) copy-start(bf16[512,512]{1,0:T(8,128)(2,1)} %query_w.1) | copy-start | bytes 1572868
  48.6 6.9 %collective-permute-start.14 = (bf16[1024,1024]{1,0:T(8,128)(2,1)}, bf16[1024,1024]{1,0:T(8,128)(2,1)}, u32[]{:S(2)}, u32[]{:S(2)}) collective-permute-start(bf16[1024,1024]{1,0:T(8,128)(2,1)} %cited_sources.3.far), channel_id=1, source_target_pairs={{0,8},{8,0},{16,24},{24,16},{32,40},{40,32},{48,56},{56,48},{64,72... | collective-permute-start | bytes 6291464 | tf_op jit(solution)/shard_map/ppermute | solution.py:41
  52.2 1.2 %copy-start.16 = (bf16[512,1024]{1,0:T(8,128)(2,1)S(1)}, bf16[512,1024]{1,0:T(8,128)(2,1)}, u32[]{:S(2)}) copy-start(bf16[512,1024]{1,0:T(8,128)(2,1)} %copy-done.15) | copy-start | bytes 3145732
  53.4 2.1 %copy-start = (s32[4,8,128,128]{3,2,1,0:T(8,128)S(1)}, s32[4,8,128,128]{3,2,1,0:T(8,128)}, u32[]{:S(2)}) copy-start(s32[4,8,128,128]{3,2,1,0:T(8,128)} %pattern_in.1) | copy-start | bytes 6291460
  53.4 2.1 %copy-start.4 = (s32[4,2,128,128]{3,2,1,0:T(8,128)S(1)}, s32[4,2,128,128]{3,2,1,0:T(8,128)}, u32[]{:S(2)}) copy-start(s32[4,2,128,128]{3,2,1,0:T(8,128)} %entity_pattern_in.1) | copy-start | bytes 1572868
  53.4 2.1 %copy-start.5 = (bf16[512,512]{1,0:T(8,128)(2,1)S(1)}, bf16[512,512]{1,0:T(8,128)(2,1)}, u32[]{:S(2)}) copy-start(bf16[512,512]{1,0:T(8,128)(2,1)} %output_w_in.1) | copy-start | bytes 1572868
  53.4 2.2 %copy-start.6 = (s32[4,8]{1,0:T(4,128)S(1)}, s32[4,8]{1,0:T(4,128)}, u32[]{:S(2)}) copy-start(s32[4,8]{1,0:T(4,128)} %tiles.1) | copy-start | bytes 388
  53.4 2.2 %copy-start.7 = (s32[4,8]{1,0:T(4,128)S(1)}, s32[4,8]{1,0:T(4,128)}, u32[]{:S(2)}) copy-start(s32[4,8]{1,0:T(4,128)} %counts.1) | copy-start | bytes 388
  53.4 2.2 %copy-start.9 = (f32[512]{0:T(512)S(1)}, f32[512]{0:T(512)}, u32[]{:S(2)}) copy-start(f32[512]{0:T(512)} %param.31) | copy-start | bytes 6148
  55.6 1.6 %copy-start.2 = (bf16[1024,1024]{1,0:T(8,128)(2,1)S(1)}, bf16[1024,1024]{1,0:T(8,128)(2,1)}, u32[]{:S(2)}) copy-start(bf16[1024,1024]{1,0:T(8,128)(2,1)} %copy-done.1) | copy-start | bytes 6291460
